TPU v7x, 32 devices: a whole 2x2x4 slice. The times are simulated.
32 devices in a mesh: dp: 8 (over z, core), tensor: 4 (over y, x).
Axes of the slice: x: 2, y: 2, z: 4, core: 2. Of those that a mesh axis runs over, the one named last changes fastest.
Arguments:
- x_quant: bfloat16 [96, 8192], P('tensor', 'dp'), may hold values from -6 to 6
- x_scale: float32 [4, 64], P('tensor', 'dp'), may hold values from 0.25 to 4
- x_outlier: int32 [4, 64], P('tensor', 'dp'), may hold values 0 or 1
- x_correction: bfloat16 [96, 8192], P('tensor', 'dp'), may hold values from -12 to 12
- g_quant: bfloat16 [96, 8192], P('tensor', 'dp'), may hold values from -6 to 6
- g_scale: float32 [4, 64], P('tensor', 'dp'), may hold values from 0.25 to 4
- g_outlier: int32 [4, 64], P('tensor', 'dp'), may hold values 0 or 1
- g_correction: bfloat16 [96, 8192], P('tensor', 'dp'), may hold values from -12 to 12
- gate_pre: bfloat16 [96, 26624], P('dp', 'tensor'), may hold values from -8 to 8
- up_pre: bfloat16 [96, 26624], P('dp', 'tensor'), may hold values from -6 to 6
- w_gate: bfloat16 [8192, 26624], P('dp', 'tensor'), may hold values from -0.0625 to 0.0625
- w_up: bfloat16 [8192, 26624], P('dp', 'tensor'), may hold values from -0.0625 to 0.0625
- w_down: bfloat16 [26624, 8192], P('tensor', 'dp'), may hold values from -0.0625 to 0.0625
Outputs:
- grad_input: bfloat16 [96, 8192], P('tensor', 'dp')
- grad_gate_weight: bfloat16 [8192, 26624], P('dp', 'tensor')
- grad_up_weight: bfloat16 [8192, 26624], P('dp', 'tensor')
- grad_down_weight: bfloat16 [26624, 8192], P('tensor', 'dp')
All inputs are finite; a program needn't handle non-finite values. No bound on the sum of `x_outlier` or of `g_outlier` on one device may be relied on, other than what follows from the above.
Results may differ from a plain program's by a relative error of at most 0.0064.
Values may be sent and summed in bfloat16 or wider, within the bound.
No kernel may reach another device: no remote copies, remote signals or barrier semaphores. Data moves between devices by JAX's collectives and lax.ppermute only.
A program may use at most 128 MiB of HBM per device.

v0:
```python
import functools
import math

import jax
import jax.numpy as jnp
from jax import lax
from jax.experimental import pallas as pl
from jax.experimental.pallas import tpu as pltpu
from jax.sharding import Mesh
from jax.sharding import PartitionSpec as P

BLK_C = 128
F32 = jnp.float32
BF16 = jnp.bfloat16
VMEM = pltpu.VMEM
SMEM = pltpu.SMEM


def after(arrays):
    return [pl.BlockSpec(memory_space=pl.ANY)] * len(arrays)


def whole(space=VMEM):
    return pl.BlockSpec(memory_space=space)


def shape(dims, dtype):
    return jax.ShapeDtypeStruct(dims, dtype)


def params(mib):
    return pltpu.CompilerParams(vmem_limit_bytes=mib * 1024 * 1024)


def cost(flops, nbytes):
    return pl.CostEstimate(flops=int(flops), bytes_accessed=int(nbytes), transcendentals=0)


def pieces(extent, step, first=0):
    cuts = [0] + list(range(first or step, extent, step)) + [extent]
    return [(a, b - a) for a, b in zip(cuts[:-1], cuts[1:])]


def prep_kernel(xq, xs, xo, xc, gq, gs, go, gc, gate, up, both, rows):
    for k, (quant, scale, flag, corr) in enumerate(((gq, gs, go, gc), (xq, xs, xo, xc))):
        for b in range(scale.shape[1]):
            cols = slice(b * BLK_C, (b + 1) * BLK_C)
            value = scale[0, b] * quant[:, cols].astype(F32) + flag[0, b].astype(F32) * corr[
                :, cols
            ].astype(F32)
            both[k, :, cols] = value.astype(BF16)
    rows[...] = jnp.concatenate([gate[...].astype(F32), up[...].astype(F32)], 0).astype(BF16)


def prep(xq, xs, xo, xc, gq, gs, go, gc, gate, up):
    rows, width = xq.shape
    tok, ff = gate.shape
    return pl.pallas_call(
        prep_kernel,
        out_shape=(shape((2, rows, width), BF16), shape((2 * tok, ff), BF16)),
        in_specs=[whole(), whole(SMEM), whole(SMEM), whole()] * 2 + [whole()] * 2,
        out_specs=(whole(),) * 2,
        compiler_params=params(56),
        cost_estimate=cost(0, 4 * xq.size * 2 + gate.size * 8),
    )(xq, xs, xo, xc, gq, gs, go, gc, gate, up)


def load_down(start, width, w_hbm, w_vmem, sems):
    copies = []
    for k, (at, size) in enumerate(pieces(width, 1024, 256)):
        first = pl.multiple_of(start + at, 16)
        copy = pltpu.make_async_copy(
            w_hbm.at[pl.ds(first, size)], w_vmem.at[pl.ds(at, size)], sems.at[k]
        )
        copy.start()
        copies.append(copy)
    return copies


def hidden_half(copies, grads_t, width, w_vmem, outs):
    rows = outs[0].shape[0]
    for copy, (at, size) in zip(copies, pieces(width, 1024, 256)):
        copy.wait()
        total = jnp.dot(w_vmem[at : at + size, :], grads_t, preferred_element_type=F32).T
        for q, out in enumerate(outs):
            out[:, at : at + size] = total[q * rows : (q + 1) * rows, :].astype(out.dtype)


def blocks_of(held, z, n_z):
    block = held.shape[0] // n_z
    return jnp.concatenate(
        [
            held[pl.ds(pl.multiple_of((z ^ m) * block, math.gcd(block, 8)), block), :]
            for m in range(n_z)
        ],
        0,
    )


def hold(parts, which, me, held):
    rows = parts[0].shape[1]
    for s, part in enumerate(parts):
        start = pl.multiple_of((me ^ s) * rows, math.gcd(rows, 8))
        held[pl.ds(start, rows), :] = part[which].astype(F32)


def first_half_kernel(n_t, n_z, offset, place, *refs):
    parts, w_hbm = refs[:n_t], refs[n_t]
    grads_out, grads_t, *outs = refs[-5 - n_z : -3]
    w_vmem, held, sems = refs[-3:]
    width = outs[0].shape[1]
    copies = load_down((1 - place[0]) * offset, width, w_hbm, w_vmem, sems)
    hold(parts, 0, place[2], held)
    grads_t[...] = held[...].T.astype(BF16)
    grads_out[...] = blocks_of(held, place[1], n_z).astype(BF16)
    hidden_half(copies, grads_t[...], width, w_vmem, outs)


def second_half_kernel(offset, place, grads_t, w_hbm, *refs):
    out, w_vmem, sems = refs[-3:]
    width = out.shape[2]
    outs = [out.at[q] for q in range(out.shape[0])]
    copies = load_down(place[0] * offset, width, w_hbm, w_vmem, sems)
    hidden_half(copies, grads_t[...], width, w_vmem, outs)


def first_half(place, parts, w_down, n_z, width, *done):
    n_t, (_, rows, chans) = len(parts), parts[0].shape
    tokens = n_t * rows
    n_copies = len(pieces(width, 1024, 256))
    return pl.pallas_call(
        functools.partial(first_half_kernel, n_t, n_z, w_down.shape[0] - width),
        out_shape=(
            shape((tokens, chans), BF16),
            shape((chans, tokens), BF16),
        )
        + (shape((tokens // n_z, width), BF16),) * n_z,
        in_specs=[whole(SMEM)] + [whole()] * n_t + [whole(pltpu.HBM)] + after(done),
        out_specs=(whole(),) * (2 + n_z),
        scratch_shapes=[
            VMEM((width, chans), BF16),
            VMEM((tokens, chans), F32),
            pltpu.SemaphoreType.DMA((n_copies,)),
        ],
        compiler_params=params(44),
        cost_estimate=cost(2 * tokens * chans * width, 2 * chans * width),
    )(place, *parts, w_down, *done)


def second_half(place, grads_t, w_down, n_z, width, *done):
    chans, tokens = grads_t.shape
    n_copies = len(pieces(width, 1024, 256))
    return pl.pallas_call(
        functools.partial(second_half_kernel, w_down.shape[0] - width),
        out_shape=shape((n_z, tokens // n_z, width), F32),
        in_specs=[whole(SMEM), whole(), whole(pltpu.HBM)] + after(done),
        out_specs=whole(),
        scratch_shapes=[VMEM((width, chans), BF16), pltpu.SemaphoreType.DMA((n_copies,))],
        compiler_params=params(44),
        cost_estimate=cost(24 * tokens * chans * width, 24 * chans * width),
    )(place, grads_t, w_down, *done)


def pair_kernel(place, mine, *refs):
    n_z = mine.shape[0]
    theirs, outs, total_ref = refs[:n_z], refs[-2 - n_z // 2 : -1], refs[-1]
    for q in range(n_z):
        total_ref[q] = mine[q] + theirs[q][...].astype(F32)
    for m in range(n_z):
        total = total_ref[place[1] ^ m]
        if m % 2:
            outs[-1][m // 2] = total.astype(BF16)
        else:
            outs[m // 2][...] = total


def pair_sum(place, mine, theirs, *done):
    n_z, rows, width = mine.shape
    return pl.pallas_call(
        pair_kernel,
        out_shape=(shape((rows, width), F32),) * (n_z // 2)
        + (shape((n_z // 2, rows, width), BF16),),
        in_specs=[whole(SMEM)] + [whole()] * (1 + n_z) + after(done),
        out_specs=(whole(),) * (n_z // 2 + 1),
        scratch_shapes=[VMEM(mine.shape, F32)],
        compiler_params=params(6),
        cost_estimate=cost(0, mine.size * 9),
    )(place, mine, *theirs, *done)


def add_kernel(picks, n_refs, *refs):
    outs = refs[-len(picks) :]
    for pick, out in zip(picks, outs):
        total = None
        for ref, row in pick:
            term = (refs[ref][...] if row is None else refs[ref][row]).astype(F32)
            total = term if total is None else total + term
        out[...] = total.astype(out.dtype)


def add_all(lists, dtypes, done=()):
    arrays, picks = [], []
    for terms in lists:
        pick = []
        for array, row in terms:
            at = next((k for k, known in enumerate(arrays) if known is array), len(arrays))
            if at == len(arrays):
                arrays.append(array)
            pick.append((at, row))
        picks.append(pick)
    dims = lists[0][0][0].shape[-2:]
    return pl.pallas_call(
        functools.partial(add_kernel, picks, len(arrays)),
        out_shape=tuple(shape(dims, dtype) for dtype in dtypes),
        in_specs=[whole()] * len(arrays) + after(done),
        out_specs=(whole(),) * len(lists),
        compiler_params=params(6),
        cost_estimate=cost(0, dims[0] * dims[1] * 6 * sum(map(len, lists))),
    )(*arrays, *done)


def sum_kernel(parts, out):
    total = parts[0].astype(F32)
    for p in range(1, parts.shape[0]):
        total = total + parts[p].astype(F32)
    out[...] = total.astype(BF16)


def sum_parts(parts):
    return pl.pallas_call(
        sum_kernel,
        out_shape=shape(parts.shape[1:], BF16),
        in_specs=[whole()],
        out_specs=whole(),
        compiler_params=params(3),
        cost_estimate=cost(0, parts.size * 3),
    )(parts)


def to_chip(value, bit, n_z):
    return lax.ppermute(value, "z", [(a, a ^ bit) for a in range(n_z)])


def to_core(value):
    return lax.ppermute(value, "core", [(0, 1), (1, 0)])


def complete_z(held, n_z):
    bit = n_z // 2
    while bit:
        for m in range(0, n_z, 2 * bit):
            if m in held and m | bit not in held:
                held[m | bit] = to_chip(held[m], bit, n_z)
        bit //= 2
    return [held[m] for m in range(n_z)]


def reduce_z(evens, odds, n_z, done):
    got = to_chip(odds, 1, n_z)
    held = {2 * k: [(even, None), (got, k)] for k, even in enumerate(evens)}
    bit = 2
    while bit < n_z:
        for m in [m for m in held if m & bit]:
            (term,) = add_all([held.pop(m)], [BF16], done[0])
            held[m ^ bit].append((to_chip(term, bit, n_z), None))
        bit *= 2
    return add_all([held[0]], [BF16], done[1])[0]


def gate_up_rows(core0, mine, theirs, cols):
    tok = mine[0].shape[0] // 2
    gate, up = [], []
    for own, other in zip(mine, theirs):
        x, y = own[:, cols].astype(F32), other[:, cols].astype(F32)
        first, second = jnp.where(core0, x, y), jnp.where(core0, y, x)
        gate += [first[:tok], second[:tok]]
        up += [first[tok:], second[tok:]]
    return jnp.concatenate(gate, 0), jnp.concatenate(up, 0)


def down_kernel(base, width, n_z, place, *refs):
    mine, theirs, grads = refs[:n_z], refs[n_z : 2 * n_z], refs[2 * n_z]
    out_hbm, token, out, sems = refs[-4:]
    token[...] = jnp.zeros_like(token)
    slots, copies = out.shape[0], []
    for k, (at, size) in enumerate(pieces(width, 512)):
        slot, cols = k % slots, slice(base + at, base + at + size)
        gate, up = gate_up_rows(place[0] == 0, mine, theirs, cols)
        hidden = gate * (1.0 / (1.0 + jnp.exp(-gate))) * up
        if k >= slots:
            copies[k - slots].wait()
        out[slot, :size, :] = jnp.dot(
            hidden.T.astype(BF16), grads[...], preferred_element_type=F32
        ).astype(BF16)
        copy = pltpu.make_async_copy(out.at[slot, :size], out_hbm.at[cols], sems.at[slot])
        copy.start()
        copies.append(copy)
    for copy in copies[-slots:]:
        copy.wait()


def down_grad(place, mine, theirs, grads, base, ff, into=None):
    n_z, total = len(mine), mine[0].shape[1]
    tokens, chans = grads.shape
    slots = min(4, len(pieces(ff, 512)))
    held = [] if into is None else [into]
    return pl.pallas_call(
        functools.partial(down_kernel, base, ff, n_z),
        out_shape=(shape((total, chans), BF16), shape((8, 128), F32)),
        in_specs=[whole(SMEM)] + [whole()] * (2 * n_z + 1) + after(held),
        out_specs=(whole(pltpu.HBM), whole()),
        scratch_shapes=[VMEM((slots, 512, chans), BF16), pltpu.SemaphoreType.DMA((slots,))],
        input_output_aliases={2 * n_z + 2: 0} if held else {},
        compiler_params=params(12),
        cost_estimate=cost(2 * tokens * chans * ff, 2 * chans * ff),
    )(place, *mine, *theirs, grads, *held)


def input_kernel(n_z, place, *refs):
    hidden, gate_up = [
        (refs[2 * k * n_z : (2 * k + 1) * n_z], refs[(2 * k + 1) * n_z : (2 * k + 2) * n_z])
        for k in range(2)
    ]
    gate_hbm, up_hbm, gate_grad, up_grad, out, w_gate, w_up, total, held, sems = refs[4 * n_z :]
    core0, z = place[0] == 0, place[1]
    rows, width = hidden[0][0].shape
    ff = gate_grad.shape[1]
    low = ff - width
    slots = w_gate.shape[0]
    parts = [(0, at, size) for at, size in pieces(low, 1024, 256)]
    parts += [(low, at, size) for at, size in pieces(width, 1024)]

    def copies(k):
        base, at, size = parts[k]
        return [
            pltpu.make_async_copy(
                hbm.at[:, base + at : base + at + size],
                vmem.at[k % slots, :, :size],
                sems.at[n, k % slots],
            )
            for n, (hbm, vmem) in enumerate(((gate_hbm, w_gate), (up_hbm, w_up)))
        ]

    def gradients(k):
        base, at, size = parts[k]
        cols, span = slice(base + at, base + at + size), slice(at, at + size)
        first = core0 if base == 0 else ~core0
        grad = jnp.concatenate(
            [
                jnp.where(first, own[:, span], other[:, span]).astype(F32)
                for own, other in zip(*hidden)
            ],
            0,
        )
        gate, up = gate_up_rows(core0, *gate_up, cols)
        sig = 1.0 / (1.0 + jnp.exp(-gate))
        gate_grad[:, cols] = (grad * up * sig * (1.0 + gate * (1.0 - sig))).astype(BF16)
        up_grad[:, cols] = (grad * (gate * sig)).astype(BF16)

    for k in range(min(slots, len(parts))):
        for copy in copies(k):
            copy.start()
    gradients(0)
    dims = (((1,), (1,)), ((), ()))
    for k, (base, at, size) in enumerate(parts):
        for copy in copies(k):
            copy.wait()
        cols, slot = slice(base + at, base + at + size), k % slots
        term = lax.dot_general(
            w_gate[slot, :, :size], gate_grad[:, cols], dims, preferred_element_type=F32
        )
        term += lax.dot_general(
            w_up[slot, :, :size], up_grad[:, cols], dims, preferred_element_type=F32
        )
        total[...] = term if k == 0 else total[...] + term
        if k + 1 < len(parts):
            gradients(k + 1)
        if k + slots < len(parts):
            for copy in copies(k + slots):
                copy.start()
    turned = total[...].T
    for m in range(n_z):
        start = pl.multiple_of((z ^ m) * rows, math.gcd(rows, 8))
        held[pl.ds(start, rows), :] = turned[m * rows : (m + 1) * rows]
    n_t = out.shape[0]
    step = held.shape[0] // n_t
    for p in range(n_t):
        out[p] = held[p * step : (p + 1) * step, :].astype(BF16)


def input_grad(place, hidden, gate_up, w_gate, w_up, n_t):
    n_z, slots = len(hidden[0]), 3
    tokens = n_z * hidden[0][0].shape[0]
    chans, ff = w_gate.shape
    return pl.pallas_call(
        functools.partial(input_kernel, n_z),
        out_shape=(shape((tokens, ff), BF16),) * 2 + (shape((n_t, tokens // n_t, chans), BF16),),
        in_specs=[whole(SMEM)] + [whole()] * (4 * n_z) + [whole(pltpu.HBM)] * 2,
        out_specs=(whole(),) * 3,
        scratch_shapes=[
            VMEM((slots, chans, min(ff, 1024)), BF16),
            VMEM((slots, chans, min(ff, 1024)), BF16),
            VMEM((chans, tokens), F32),
            VMEM((tokens, chans), F32),
            pltpu.SemaphoreType.DMA((2, slots)),
        ],
        compiler_params=params(42),
        cost_estimate=cost(4 * tokens * chans * ff, 4 * chans * ff + 12 * tokens * ff),
    )(place, *hidden[0], *hidden[1], *gate_up[0], *gate_up[1], w_gate, w_up)


def weight_kernel(n_z, n_t, place, *refs):
    gate_grad, up_grad, gate_hbm, up_hbm, out, held, inputs_t, sems = refs[n_t:]
    hold(refs[:n_t], 1, place[2], held)
    inputs_t[...] = blocks_of(held, place[1], n_z).T.astype(BF16)
    copies = []
    ff, slots = gate_grad.shape[1], out.shape[0]
    for grad, hbm in ((gate_grad, gate_hbm), (up_grad, up_hbm)):
        for at, size in pieces(ff, 512):
            cols, slot = slice(at, at + size), len(copies) % slots
            if len(copies) >= slots:
                copies[len(copies) - slots].wait()
            out[slot, :, :size] = jnp.dot(
                inputs_t[...], grad[:, cols], preferred_element_type=F32
            ).astype(BF16)
            copy = pltpu.make_async_copy(out.at[slot, :, :size], hbm.at[:, cols], sems.at[slot])
            copy.start()
            copies.append(copy)
    for copy in copies[-slots:]:
        copy.wait()


def weight_grads(place, parts, gate_grad, up_grad, n_z):
    n_t, chans, tokens = len(parts), parts[0].shape[2], gate_grad.shape[0]
    ff = gate_grad.shape[1]
    slots = min(8, 2 * len(pieces(ff, 512)))
    return pl.pallas_call(
        functools.partial(weight_kernel, n_z, n_t),
        out_shape=(shape((chans, ff), BF16),) * 2,
        in_specs=[whole(SMEM)] + [whole()] * (n_t + 2),
        out_specs=(whole(pltpu.HBM),) * 2,
        scratch_shapes=[
            VMEM((slots, chans, 512), BF16),
            VMEM((tokens, chans), F32),
            VMEM((chans, tokens), BF16),
            pltpu.SemaphoreType.DMA((slots,)),
        ],
        compiler_params=params(16),
        cost_estimate=cost(4 * tokens * chans * ff, 4 * chans * ff + 4 * tokens * ff),
    )(place, *parts, gate_grad, up_grad)


def on_device(n_z, n_t, xq, xs, xo, xc, gq, gs, go, gc, gate_pre, up_pre, w_gate, w_up, w_down):
    place = jnp.stack([lax.axis_index(name) for name in ("core", "z", "tensor")]).astype(jnp.int32)
    ff = gate_pre.shape[1]
    width = -(-ff // 256) * 128

    def from_tensor(own):
        return [own] + [
            lax.ppermute(own, "tensor", [(a, a ^ s) for a in range(n_t)]) for s in range(1, n_t)
        ]

    both, rows = prep(xq, xs, xo, xc, gq, gs, go, gc, gate_pre, up_pre)
    both = from_tensor(both)
    bit = n_z // 2
    rows = {0: rows, bit: to_chip(rows, bit, n_z), 1: to_chip(rows, 1, n_z)}
    grads, grads_t, *send = first_half(place, both, w_down, n_z, width)
    got = [to_core(part) for part in send]
    mine = second_half(place, grads_t, w_down, n_z, width, rows[1], rows[bit])
    rows[bit | 1] = to_chip(rows[bit], 1, n_z)
    *evens, odds = pair_sum(place, mine, got, rows[bit | 1])
    rows = complete_z(rows, n_z)
    gate_up = (rows, [to_core(part) for part in rows])
    grad_down, token = down_grad(place, *gate_up, grads, 0, ff - width)
    hidden = {0: reduce_z(evens, odds, n_z, (gate_up[1], [token]))}
    hidden |= {bit: to_chip(hidden[0], bit, n_z), 1: to_chip(hidden[0], 1, n_z)}
    grad_down, token = down_grad(place, *gate_up, grads, ff - width, width, grad_down)
    (hidden[bit],) = add_all([[(hidden[bit], None)]], [BF16], [token, hidden[1]])
    hidden = complete_z(hidden, n_z)
    gate_grad, up_grad, sends = input_grad(
        place, (hidden, [to_core(part) for part in hidden]), gate_up, w_gate, w_up, n_t
    )
    terms = lax.all_to_all(sends, "tensor", 0, 0, tiled=True)
    grad_gate, grad_up = weight_grads(place, both, gate_grad, up_grad, n_z)
    return sum_parts(terms), grad_gate, grad_up, grad_down


def solution(mesh):
    n_dp, n_t = mesh.shape["dp"], mesh.shape["tensor"]
    fine = Mesh(mesh.devices.reshape(n_dp // 2, 2, n_t), ("z", "core", "tensor"))
    by_token, by_dp = P("tensor", ("z", "core")), P(("z", "core"), "tensor")
    return jax.shard_map(
        functools.partial(on_device, n_dp // 2, n_t),
        mesh=fine,
        in_specs=(by_token,) * 8 + (by_dp,) * 4 + (by_token,),
        out_specs=(by_token, by_dp, by_dp, by_token),
        check_vma=False,
    )
```

profile of v0, /device:TPU:0, one launch (start us, length us, event | category | flops | bytes accessed | tf_op | source)
XLA Modules:
  0.0 103.5 jit_solution(1545471240074722319)
XLA Ops:
  0.6 2.0 %shard_map.156 = (bf16[2,24,1024]{2,1,0:T(8,128)(2,1)}, bf16[24,6656]{1,0:T(8,128)(2,1)}) custom-call(bf16[24,1024]{1,0:T(8,128)(2,1)} %xq.1, f32[1,8]{1,0:T(1,128)} %xs.1, s32[1,8]{1,0:T(1,128)} %xo.1, bf16[24,1024]{1,0:T(8,128)(2,1)} %xc.1, bf16[24,1024]{1,0:T(8,128)(2,1)} %gq.1, f32[1,8]{1,0:T(1,128)} %gs.1, s32[1,8]{1,0:T(1,128)} %go.1, ...), custom_call_target="tpu_custom_call" | custom-call | bytes 835584 | tf_op jit(solution)/shard_map/pallas_call | solution.py:58
  2.6 4.0 %collective-permute-start.4 = (bf16[24,6656]{1,0:T(8,128)(2,1)}, bf16[24,6656]{1,0:T(8,128)(2,1)S(1)}, u32[]{:S(2)}, u32[]{:S(2)}) collective-permute-start(bf16[24,6656]{1,0:T(8,128)(2,1)} %get-tuple-element.26.refs_0_.refs_8_), channel_id=1, source_target_pairs={{0,16},{8,24},{16,0},{24,8},{1,17},{9,25},{17,1},{25,9},{2,18},{10... | collective-permute-start | bytes 958472 | tf_op jit(solution)/shard_map/ppermute | solution.py:241
  6.7 1.6 %collective-permute-start.3 = (bf16[24,6656]{1,0:T(8,128)(2,1)}, bf16[24,6656]{1,0:T(8,128)(2,1)S(1)}, u32[]{:S(2)}, u32[]{:S(2)}) collective-permute-start(bf16[24,6656]{1,0:T(8,128)(2,1)} %get-tuple-element.26.refs_0_.refs_8_), channel_id=1, source_target_pairs={{0,8},{8,0},{16,24},{24,16},{1,9},{9,1},{17,25},{25,17},{2,10},{10... | collective-permute-start | bytes 958472 | tf_op jit(solution)/shard_map/ppermute | solution.py:241
  8.2 2.4 %collective-permute-start.2 = (bf16[2,24,1024]{2,1,0:T(8,128)(2,1)}, bf16[2,24,1024]{2,1,0:T(8,128)(2,1)S(1)}, u32[]{:S(2)}, u32[]{:S(2)}) collective-permute-start(bf16[2,24,1024]{2,1,0:T(8,128)(2,1)} %get-tuple-element.24.refs_0_), channel_id=1, source_target_pairs={{0,3},{1,2},{2,1},{3,0},{4,7},{5,6},{6,5},{7,4},{8,11},{9,10},{10,... | collective-permute-start | bytes 294920 | tf_op jit(solution)/shard_map/ppermute | solution.py:460
  11.8 2.5 %collective-permute-done.2.refs_3_ = bf16[2,24,1024]{2,1,0:T(8,128)(2,1)S(1)} collective-permute-done((bf16[2,24,1024]{2,1,0:T(8,128)(2,1)}, bf16[2,24,1024]{2,1,0:T(8,128)(2,1)S(1)}, u32[]{:S(2)}, u32[]{:S(2)}) %collective-permute-start.2) | collective-permute-done | bytes 98336 | tf_op jit(solution)/shard_map/ppermute | solution.py:460
  14.3 1.3 %collective-permute-done.1.refs_2_ = bf16[2,24,1024]{2,1,0:T(8,128)(2,1)S(1)} collective-permute-done((bf16[2,24,1024]{2,1,0:T(8,128)(2,1)}, bf16[2,24,1024]{2,1,0:T(8,128)(2,1)S(1)}, u32[]{:S(2)}, u32[]{:S(2)}) %collective-permute-start.1) | collective-permute-done | bytes 98336 | tf_op jit(solution)/shard_map/ppermute | solution.py:460
  16.0 0.9 copy-done.1
  16.9 5.7 %shard_map.157 = (bf16[96,1024]{1,0:T(8,128)(2,1)S(1)}, bf16[1024,96]{1,0:T(8,128)(2,1)S(1)}, bf16[24,3328]{1,0:T(8,128)(2,1)S(1)}, bf16[24,3328]{1,0:T(8,128)(2...) custom-call(s32[3]{0:T(128)S(1)} %pad_add_fusion.place, bf16[2,24,1024]{2,1,0:T(8,128)(2,1)S(1)} %copy-done.1, ...), custom_call_target="tpu_custom_call" | custom-call | flops 654311424 | bytes 6815744 | tf_op jit(solution)/shard_map/pallas_call | solution.py:131
  24.2 5.7 %shard_map.158.mine = f32[4,24,3328]{2,1,0:T(8,128)S(1)} custom-call(s32[3]{0:T(128)S(1)} %pad_add_fusion.place, bf16[1024,96]{1,0:T(8,128)(2,1)S(1)} %get-tuple-element.25.grads_t, bf16[6656,1024]{1,0:T(8,128)(2,1)} %w_hbm.1, bf16[24,6656]{1,0:T(8,128)(2,1)S(1)} %collective-permute-done.3.refs_0_.refs_1_.refs_9_, ...), custom_call_target="tpu_custom_call" | custom-call | flops 7851737088 | bytes 81788928 | tf_op jit(solution)/shard_map/pallas_call | solution.py:153
  30.6 2.7 %collective-permute-done.9.refs_4_.refs_3_.refs_11_ = bf16[24,6656]{1,0:T(8,128)(2,1)S(1)} collective-permute-done((bf16[24,6656]{1,0:T(8,128)(2,1)S(1)}, bf16[24,6656]{1,0:T(8,128)(2,1)S(1)}, u32[]{:S(2)}, u32[]{:S(2)}) %collective-permute-start.9) | collective-permute-done | bytes 319520 | tf_op jit(solution)/shard_map/ppermute | solution.py:241
  33.3 0.7 shard_map.159
  34.9 9.1 %collective-permute-done.10.refs_1_ = bf16[2,24,3328]{2,1,0:T(8,128)(2,1)S(1)} collective-permute-done((bf16[2,24,3328]{2,1,0:T(8,128)(2,1)S(1)}, bf16[2,24,3328]{2,1,0:T(8,128)(2,1)S(1)}, u32[]{:S(2)}, u32[]{:S(2)}) %collective-permute-start.10) | collective-permute-done | bytes 319520 | tf_op jit(solution)/shard_map/ppermute | solution.py:241
  44.5 4.2 %shard_map.161 = (bf16[6656,1024]{1,0:T(8,128)(2,1)}, f32[8,128]{1,0:T(8,128)S(1)}) custom-call(s32[3]{0:T(128)S(1)} %pad_add_fusion.place, bf16[24,6656]{1,0:T(8,128)(2,1)S(1)} %copy-done, bf16[24,6656]{1,0:T(8,128)(2,1)S(1)} %collective-permute-done.3.refs_0_.refs_1_.refs_9_, bf16[24,6656]{1,0:T(8,128)(2,1)S(1)} %collective-permute-done.4.refs_1_.refs_2_.refs_10_, ...), custom_call_target="tpu_custom_call" | custom-call | flops 654311424 | bytes 6815744 | tf_op jit(solution)/shard_map/pallas_call | solution.py:307
  48.6 5.4 %collective-permute-done.15.refs_2_ = bf16[24,3328]{1,0:T(8,128)(2,1)S(1)} collective-permute-done((bf16[24,3328]{1,0:T(8,128)(2,1)S(1)}, bf16[24,3328]{1,0:T(8,128)(2,1)S(1)}, u32[]{:S(2)}, u32[]{:S(2)}) %collective-permute-start.15) | collective-permute-done | bytes 159776 | tf_op jit(solution)/shard_map/ppermute | solution.py:241
  54.2 1.9 %collective-permute-start.16 = (bf16[24,3328]{1,0:T(8,128)(2,1)S(1)}, bf16[24,3328]{1,0:T(8,128)(2,1)S(1)}, u32[]{:S(2)}, u32[]{:S(2)}) collective-permute-start(bf16[24,3328]{1,0:T(8,128)(2,1)S(1)} %shard_map.162.refs_0_), channel_id=1, source_target_pairs={{0,8},{8,0},{16,24},{24,16},{1,9},{9,1},{17,25},{25,17},{2,10},{10... | collective-permute-start | bytes 479240 | tf_op jit(solution)/shard_map/ppermute | solution.py:241
  56.1 4.2 %shard_map.163 = (bf16[6656,1024]{1,0:T(8,128)(2,1)}, f32[8,128]{1,0:T(8,128)S(1)}) custom-call(s32[3]{0:T(128)S(1)} %pad_add_fusion.place, bf16[24,6656]{1,0:T(8,128)(2,1)S(1)} %copy-done, bf16[24,6656]{1,0:T(8,128)(2,1)S(1)} %collective-permute-done.3.refs_0_.refs_1_.refs_9_, ...), custom_call_target="tpu_custom_call", output_to_operand_aliasing={{0}: (10, {})} | custom-call | flops 654311424 | bytes 6815744 | tf_op jit(solution)/shard_map/pallas_call | solution.py:307
  60.3 3.1 %collective-permute-done.17.refs_0_ = bf16[24,3328]{1,0:T(8,128)(2,1)S(1)} collective-permute-done((bf16[24,3328]{1,0:T(8,128)(2,1)S(1)}, bf16[24,3328]{1,0:T(8,128)(2,1)S(1)}, u32[]{:S(2)}, u32[]{:S(2)}) %collective-permute-start.17) | collective-permute-done | bytes 159776 | tf_op jit(solution)/shard_map/ppermute | solution.py:241
  64.6 4.9 %collective-permute-done.18.refs_3_ = bf16[24,3328]{1,0:T(8,128)(2,1)S(1)} collective-permute-done((bf16[24,3328]{1,0:T(8,128)(2,1)S(1)}, bf16[24,3328]{1,0:T(8,128)(2,1)S(1)}, u32[]{:S(2)}, u32[]{:S(2)}) %collective-permute-start.18) | collective-permute-done | bytes 159776 | tf_op jit(solution)/shard_map/ppermute | solution.py:241
  69.5 1.4 %collective-permute-done.22.refs_7_ = bf16[24,3328]{1,0:T(8,128)(2,1)S(1)} collective-permute-done((bf16[24,3328]{1,0:T(8,128)(2,1)S(1)}, bf16[24,3328]{1,0:T(8,128)(2,1)S(1)}, u32[]{:S(2)}, u32[]{:S(2)}) %collective-permute-start.22) | collective-permute-done | bytes 159776 | tf_op jit(solution)/shard_map/ppermute | solution.py:245
  70.8 14.4 %shard_map.165 = (bf16[96,6656]{1,0:T(8,128)(2,1)S(1)}, bf16[96,6656]{1,0:T(8,128)(2,1)S(1)}, bf16[4,24,1024]{2,1,0:T(8,128)(2,1)}) custom-call(s32[3]{0:T(128)S(1)} %pad_add_fusion.place, bf16[24,3328]{1,0:T(8,128)(2,1)S(1)} %shard_map.162.refs_0_, bf16[24,3328]{1,0:T(8,128)(2,1)S(1)} %collective-permute-done.16.refs_2_.refs_1_, ...), custom_call_target="tpu_custom_call" | custom-call | flops 2617245696 | bytes 34930688 | tf_op jit(solution)/shard_map/pallas_call | solution.py:395
  85.3 1.0 %copy-done.3 = bf16[96,6656]{1,0:T(8,128)(2,1)} copy-done((bf16[96,6656]{1,0:T(8,128)(2,1)}, bf16[96,6656]{1,0:T(8,128)(2,1)S(1)}, u32[]{:S(2)}) %copy-start.3) | copy-done | bytes 1277976
  86.3 3.7 %all-to-all-start = ((bf16[4,24,1024]{2,1,0:T(8,128)(2,1)}), bf16[4,24,1024]{2,1,0:T(8,128)(2,1)S(1)}, u32[]{:S(2)}, u32[]{:S(2)}) async-start(bf16[4,24,1024]{2,1,0:T(8,128)(2,1)} %get-tuple-element.38), calls=%async_computation | async-start | bytes 393216 | tf_op jit(solution)/shard_map/all_to_all | solution.py:483
  90.0 1.3 %copy-done.4 = bf16[96,6656]{1,0:T(8,128)(2,1)S(1)} copy-done((bf16[96,6656]{1,0:T(8,128)(2,1)S(1)}, bf16[96,6656]{1,0:T(8,128)(2,1)}, u32[]{:S(2)}) %copy-start.4) | copy-done | bytes 1277976
  91.3 11.5 %shard_map.167 = (bf16[1024,6656]{1,0:T(8,128)(2,1)}, bf16[1024,6656]{1,0:T(8,128)(2,1)}) custom-call(s32[3]{0:T(128)S(1)} %pad_add_fusion.place, bf16[2,24,1024]{2,1,0:T(8,128)(2,1)S(1)} %copy-done.2, bf16[2,24,1024]{2,1,0:T(8,128)(2,1)S(1)} %collective-permute-done.refs_1_, bf16[2,24,1024]{2,1,0:T(8,128)(2,1)S(1)} %collective-permute-done.1.refs_2_, ...), custom_call_target="tpu_custom_call" | custom-call | flops 2617245696 | bytes 29818880 | tf_op jit(solution)/shard_map/pallas_call | solution.py:437
  (47 shorter events, 7.0 us)
Async XLA Ops:
  2.6 20.7 %collective-permute-start.4 = (bf16[24,6656]{1,0:T(8,128)(2,1)}, bf16[24,6656]{1,0:T(8,128)(2,1)S(1)}, u32[]{:S(2)}, u32[]{:S(2)}) collective-permute-start(bf16[24,6656]{1,0:T(8,128)(2,1)} %get-tuple-element.26.refs_0_.refs_8_), channel_id=1, source_target_pairs={{0,16},{8,24},{16,0},{24,8},{1,17},{9,25},{17,1},{25,9},{2,18},{10... | collective-permute-start | bytes 958472 | tf_op jit(solution)/shard_map/ppermute | solution.py:241
  6.7 17.1 %collective-permute-start.3 = (bf16[24,6656]{1,0:T(8,128)(2,1)}, bf16[24,6656]{1,0:T(8,128)(2,1)S(1)}, u32[]{:S(2)}, u32[]{:S(2)}) collective-permute-start(bf16[24,6656]{1,0:T(8,128)(2,1)} %get-tuple-element.26.refs_0_.refs_8_), channel_id=1, source_target_pairs={{0,8},{8,0},{16,24},{24,16},{1,9},{9,1},{17,25},{25,17},{2,10},{10... | collective-permute-start | bytes 958472 | tf_op jit(solution)/shard_map/ppermute | solution.py:241
  8.2 6.1 %collective-permute-start.2 = (bf16[2,24,1024]{2,1,0:T(8,128)(2,1)}, bf16[2,24,1024]{2,1,0:T(8,128)(2,1)S(1)}, u32[]{:S(2)}, u32[]{:S(2)}) collective-permute-start(bf16[2,24,1024]{2,1,0:T(8,128)(2,1)} %get-tuple-element.24.refs_0_), channel_id=1, source_target_pairs={{0,3},{1,2},{2,1},{3,0},{4,7},{5,6},{6,5},{7,4},{8,11},{9,10},{10,... | collective-permute-start | bytes 294920 | tf_op jit(solution)/shard_map/ppermute | solution.py:460
  10.7 5.0 %collective-permute-start.1 = (bf16[2,24,1024]{2,1,0:T(8,128)(2,1)}, bf16[2,24,1024]{2,1,0:T(8,128)(2,1)S(1)}, u32[]{:S(2)}, u32[]{:S(2)}) collective-permute-start(bf16[2,24,1024]{2,1,0:T(8,128)(2,1)} %get-tuple-element.24.refs_0_), channel_id=1, source_target_pairs={{0,2},{1,3},{2,0},{3,1},{4,6},{5,7},{6,4},{7,5},{8,10},{9,11},{10,... | collective-permute-start | bytes 294920 | tf_op jit(solution)/shard_map/ppermute | solution.py:460
  11.2 4.8 %collective-permute-start = (bf16[2,24,1024]{2,1,0:T(8,128)(2,1)}, bf16[2,24,1024]{2,1,0:T(8,128)(2,1)S(1)}, u32[]{:S(2)}, u32[]{:S(2)}) collective-permute-start(bf16[2,24,1024]{2,1,0:T(8,128)(2,1)} %get-tuple-element.24.refs_0_), channel_id=1, source_target_pairs={{0,1},{1,0},{2,3},{3,2},{4,5},{5,4},{6,7},{7,6},{8,9},{9,8},{10,11... | collective-permute-start | bytes 294920 | tf_op jit(solution)/shard_map/ppermute | solution.py:460
  22.6 7.2 %collective-permute-start.5 = (bf16[24,3328]{1,0:T(8,128)(2,1)S(1)}, bf16[24,3328]{1,0:T(8,128)(2,1)S(1)}, u32[]{:S(2)}, u32[]{:S(2)}) collective-permute-start(bf16[24,3328]{1,0:T(8,128)(2,1)S(1)} %get-tuple-element.27), channel_id=1, source_target_pairs={{0,4},{4,0},{1,5},{5,1},{2,6},{6,2},{3,7},{7,3},{8,12},{12,8},{9,1... | collective-permute-start | bytes 479240 | tf_op jit(solution)/shard_map/ppermute | solution.py:245
  22.7 7.3 %collective-permute-start.6 = (bf16[24,3328]{1,0:T(8,128)(2,1)S(1)}, bf16[24,3328]{1,0:T(8,128)(2,1)S(1)}, u32[]{:S(2)}, u32[]{:S(2)}) collective-permute-start(bf16[24,3328]{1,0:T(8,128)(2,1)S(1)} %get-tuple-element.28), channel_id=1, source_target_pairs={{0,4},{4,0},{1,5},{5,1},{2,6},{6,2},{3,7},{7,3},{8,12},{12,8},{9,1... | collective-permute-start | bytes 479240 | tf_op jit(solution)/shard_map/ppermute | solution.py:245
  23.2 7.3 %collective-permute-start.7 = (bf16[24,3328]{1,0:T(8,128)(2,1)S(1)}, bf16[24,3328]{1,0:T(8,128)(2,1)S(1)}, u32[]{:S(2)}, u32[]{:S(2)}) collective-permute-start(bf16[24,3328]{1,0:T(8,128)(2,1)S(1)} %get-tuple-element.29), channel_id=1, source_target_pairs={{0,4},{4,0},{1,5},{5,1},{2,6},{6,2},{3,7},{7,3},{8,12},{12,8},{9,1... | collective-permute-start | bytes 479240 | tf_op jit(solution)/shard_map/ppermute | solution.py:245
  23.3 10.0 %collective-permute-start.8 = (bf16[24,3328]{1,0:T(8,128)(2,1)S(1)}, bf16[24,3328]{1,0:T(8,128)(2,1)S(1)}, u32[]{:S(2)}, u32[]{:S(2)}) collective-permute-start(bf16[24,3328]{1,0:T(8,128)(2,1)S(1)} %get-tuple-element.30), channel_id=1, source_target_pairs={{0,4},{4,0},{1,5},{5,1},{2,6},{6,2},{3,7},{7,3},{8,12},{12,8},{9,1... | collective-permute-start | bytes 479240 | tf_op jit(solution)/shard_map/ppermute | solution.py:245
  23.7 9.5 %collective-permute-start.9 = (bf16[24,6656]{1,0:T(8,128)(2,1)S(1)}, bf16[24,6656]{1,0:T(8,128)(2,1)S(1)}, u32[]{:S(2)}, u32[]{:S(2)}) collective-permute-start(bf16[24,6656]{1,0:T(8,128)(2,1)S(1)} %collective-permute-done.4.refs_1_.refs_2_.refs_10_), channel_id=1, source_target_pairs={{0,8},{8,0},{16,24},{24,16},{1,9},{9,1},{17,25},{25,17},{2,10},{10... | collective-permute-start | bytes 958472 | tf_op jit(solution)/shard_map/ppermute | solution.py:241
  29.9 4.6 %collective-permute-start.11 = (bf16[24,6656]{1,0:T(8,128)(2,1)S(1)}, bf16[24,6656]{1,0:T(8,128)(2,1)S(1)}, u32[]{:S(2)}, u32[]{:S(2)}) collective-permute-start(bf16[24,6656]{1,0:T(8,128)(2,1)S(1)} %copy-done), channel_id=1, source_target_pairs={{0,4},{4,0},{1,5},{5,1},{2,6},{6,2},{3,7},{7,3},{8,12},{12,8},{9,1... | collective-permute-start | bytes 958472 | tf_op jit(solution)/shard_map/ppermute | solution.py:245
  30.0 4.5 %collective-permute-start.13 = (bf16[24,6656]{1,0:T(8,128)(2,1)S(1)}, bf16[24,6656]{1,0:T(8,128)(2,1)S(1)}, u32[]{:S(2)}, u32[]{:S(2)}) collective-permute-start(bf16[24,6656]{1,0:T(8,128)(2,1)S(1)} %collective-permute-done.4.refs_1_.refs_2_.refs_10_), channel_id=1, source_target_pairs={{0,4},{4,0},{1,5},{5,1},{2,6},{6,2},{3,7},{7,3},{8,12},{12,8},{9,1... | collective-permute-start | bytes 958472 | tf_op jit(solution)/shard_map/ppermute | solution.py:245
  30.5 4.0 %collective-permute-start.12 = (bf16[24,6656]{1,0:T(8,128)(2,1)S(1)}, bf16[24,6656]{1,0:T(8,128)(2,1)S(1)}, u32[]{:S(2)}, u32[]{:S(2)}) collective-permute-start(bf16[24,6656]{1,0:T(8,128)(2,1)S(1)} %collective-permute-done.3.refs_0_.refs_1_.refs_9_), channel_id=1, source_target_pairs={{0,4},{4,0},{1,5},{5,1},{2,6},{6,2},{3,7},{7,3},{8,12},{12,8},{9,1... | collective-permute-start | bytes 958472 | tf_op jit(solution)/shard_map/ppermute | solution.py:245
  33.3 1.6 %collective-permute-start.14 = (bf16[24,6656]{1,0:T(8,128)(2,1)S(1)}, bf16[24,6656]{1,0:T(8,128)(2,1)S(1)}, u32[]{:S(2)}, u32[]{:S(2)}) collective-permute-start(bf16[24,6656]{1,0:T(8,128)(2,1)S(1)} %collective-permute-done.9.refs_4_.refs_3_.refs_11_), channel_id=1, source_target_pairs={{0,4},{4,0},{1,5},{5,1},{2,6},{6,2},{3,7},{7,3},{8,12},{12,8},{9,1... | collective-permute-start | bytes 958472 | tf_op jit(solution)/shard_map/ppermute | solution.py:245
  34.0 10.0 %collective-permute-start.10 = (bf16[2,24,3328]{2,1,0:T(8,128)(2,1)S(1)}, bf16[2,24,3328]{2,1,0:T(8,128)(2,1)S(1)}, u32[]{:S(2)}, u32[]{:S(2)}) collective-permute-start(bf16[2,24,3328]{2,1,0:T(8,128)(2,1)S(1)} %get-tuple-element.32), channel_id=1, source_target_pairs={{0,8},{8,0},{16,24},{24,16},{1,9},{9,1},{17,25},{25,17},{2,10},{10... | collective-permute-start | bytes 958472 | tf_op jit(solution)/shard_map/ppermute | solution.py:241
  44.1 10.0 %collective-permute-start.15 = (bf16[24,3328]{1,0:T(8,128)(2,1)S(1)}, bf16[24,3328]{1,0:T(8,128)(2,1)S(1)}, u32[]{:S(2)}, u32[]{:S(2)}) collective-permute-start(bf16[24,3328]{1,0:T(8,128)(2,1)S(1)} %shard_map.160), channel_id=1, source_target_pairs={{0,16},{8,24},{16,0},{24,8},{1,17},{9,25},{17,1},{25,9},{2,18},{10... | collective-permute-start | bytes 479240 | tf_op jit(solution)/shard_map/ppermute | solution.py:241
  54.1 9.2 %collective-permute-start.17 = (bf16[24,3328]{1,0:T(8,128)(2,1)S(1)}, bf16[24,3328]{1,0:T(8,128)(2,1)S(1)}, u32[]{:S(2)}, u32[]{:S(2)}) collective-permute-start(bf16[24,3328]{1,0:T(8,128)(2,1)S(1)} %shard_map.162.refs_0_), channel_id=1, source_target_pairs={{0,16},{8,24},{16,0},{24,8},{1,17},{9,25},{17,1},{25,9},{2,18},{10... | collective-permute-start | bytes 479240 | tf_op jit(solution)/shard_map/ppermute | solution.py:241
  54.2 9.5 %collective-permute-start.16 = (bf16[24,3328]{1,0:T(8,128)(2,1)S(1)}, bf16[24,3328]{1,0:T(8,128)(2,1)S(1)}, u32[]{:S(2)}, u32[]{:S(2)}) collective-permute-start(bf16[24,3328]{1,0:T(8,128)(2,1)S(1)} %shard_map.162.refs_0_), channel_id=1, source_target_pairs={{0,8},{8,0},{16,24},{24,16},{1,9},{9,1},{17,25},{25,17},{2,10},{10... | collective-permute-start | bytes 479240 | tf_op jit(solution)/shard_map/ppermute | solution.py:241
  63.8 5.7 %collective-permute-start.18 = (bf16[24,3328]{1,0:T(8,128)(2,1)S(1)}, bf16[24,3328]{1,0:T(8,128)(2,1)S(1)}, u32[]{:S(2)}, u32[]{:S(2)}) collective-permute-start(bf16[24,3328]{1,0:T(8,128)(2,1)S(1)} %shard_map.164.refs_2_), channel_id=1, source_target_pairs={{0,8},{8,0},{16,24},{24,16},{1,9},{9,1},{17,25},{25,17},{2,10},{10... | collective-permute-start | bytes 479240 | tf_op jit(solution)/shard_map/ppermute | solution.py:241
  64.1 5.4 %collective-permute-start.19 = (bf16[24,3328]{1,0:T(8,128)(2,1)S(1)}, bf16[24,3328]{1,0:T(8,128)(2,1)S(1)}, u32[]{:S(2)}, u32[]{:S(2)}) collective-permute-start(bf16[24,3328]{1,0:T(8,128)(2,1)S(1)} %shard_map.162.refs_0_), channel_id=1, source_target_pairs={{0,4},{4,0},{1,5},{5,1},{2,6},{6,2},{3,7},{7,3},{8,12},{12,8},{9,1... | collective-permute-start | bytes 479240 | tf_op jit(solution)/shard_map/ppermute | solution.py:245
  64.1 5.4 %collective-permute-start.21 = (bf16[24,3328]{1,0:T(8,128)(2,1)S(1)}, bf16[24,3328]{1,0:T(8,128)(2,1)S(1)}, u32[]{:S(2)}, u32[]{:S(2)}) collective-permute-start(bf16[24,3328]{1,0:T(8,128)(2,1)S(1)} %shard_map.164.refs_2_), channel_id=1, source_target_pairs={{0,4},{4,0},{1,5},{5,1},{2,6},{6,2},{3,7},{7,3},{8,12},{12,8},{9,1... | collective-permute-start | bytes 479240 | tf_op jit(solution)/shard_map/ppermute | solution.py:245
  64.6 4.9 %collective-permute-start.20 = (bf16[24,3328]{1,0:T(8,128)(2,1)S(1)}, bf16[24,3328]{1,0:T(8,128)(2,1)S(1)}, u32[]{:S(2)}, u32[]{:S(2)}) collective-permute-start(bf16[24,3328]{1,0:T(8,128)(2,1)S(1)} %collective-permute-done.16.refs_2_.refs_1_), channel_id=1, source_target_pairs={{0,4},{4,0},{1,5},{5,1},{2,6},{6,2},{3,7},{7,3},{8,12},{12,8},{9,1... | collective-permute-start | bytes 479240 | tf_op jit(solution)/shard_map/ppermute | solution.py:245
  69.4 1.4 %collective-permute-start.22 = (bf16[24,3328]{1,0:T(8,128)(2,1)S(1)}, bf16[24,3328]{1,0:T(8,128)(2,1)S(1)}, u32[]{:S(2)}, u32[]{:S(2)}) collective-permute-start(bf16[24,3328]{1,0:T(8,128)(2,1)S(1)} %collective-permute-done.18.refs_3_), channel_id=1, source_target_pairs={{0,4},{4,0},{1,5},{5,1},{2,6},{6,2},{3,7},{7,3},{8,12},{12,8},{9,1... | collective-permute-start | bytes 479240 | tf_op jit(solution)/shard_map/ppermute | solution.py:245
  86.3 16.5 %all-to-all-start = ((bf16[4,24,1024]{2,1,0:T(8,128)(2,1)}), bf16[4,24,1024]{2,1,0:T(8,128)(2,1)S(1)}, u32[]{:S(2)}, u32[]{:S(2)}) async-start(bf16[4,24,1024]{2,1,0:T(8,128)(2,1)} %get-tuple-element.38), calls=%async_computation | async-start | bytes 393216 | tf_op jit(solution)/shard_map/all_to_all | solution.py:483
  (5 other events, 35.2 us)
where the time goes:
time: 104 us; the launch traced here: 103 us
  Pallas kernels  49.1 us (47%)
  waiting for transfers between devices  31.5 us (30%)
  starting transfers between devices  18.7 us (18%)
  local copies, waits for them, and re-layouts  3.25 us (3%)
    ppermute x8, waiting for transfers between devices, to_chip(): return lax.ppermute(value, 'z', [(a, a ^ bit) for a in range(n_z)])  25.6 us
    pallas_call x1, Pallas kernels, input_grad(): pl.pallas_call(functools.partial(input_kernel, n_z), out_shape=(shape((to...  14.4 us
    pallas_call x1, Pallas kernels, weight_grads(): pl.pallas_call(functools.partial(weight_kernel, n_z, n_t), out_shape=(sha...  11.5 us
    ppermute x8, starting transfers between devices, to_chip(): return lax.ppermute(value, 'z', [(a, a ^ bit) for a in range(n_z)])  9.26 us
    pallas_call x2, Pallas kernels, down_grad(): pl.pallas_call(functools.partial(down_kernel, base, ff, n_z), out_shape=(...  8.31 us
    pallas_call x1, Pallas kernels, first_half(): pl.pallas_call(functools.partial(first_half_kernel, n_t, n_z, w_down.shap...  5.73 us
    pallas_call x1, Pallas kernels, second_half(): pl.pallas_call(functools.partial(second_half_kernel, w_down.shape[0] - wi...  5.69 us
    ppermute x3, waiting for transfers between devices, from_tensor(): lax.ppermute(own, 'tensor', [(a, a ^ s) for a in range(n_t)])  4.21 us
  transfers between devices with their start and end apart: 24, of which 11 were waited for; matrix products, arithmetic and copies ran while one was open for 0% of the time, Pallas kernels for 31%

commit v1 on v0

--- a/solution.py
+++ b/solution.py
@@ -77,13 +77,27 @@
     return copies
 
 
-def hidden_half(copies, grads_t, width, w_vmem, outs):
-    rows = outs[0].shape[0]
-    for copy, (at, size) in zip(copies, pieces(width, 1024, 256)):
-        copy.wait()
-        total = jnp.dot(w_vmem[at : at + size, :], grads_t, preferred_element_type=F32).T
+def hidden_half(copies, grads_t, width, w_vmem, outs, turned):
+    rows, depth = outs[0].shape[0], grads_t.shape[0] // 2
+
+    def put(k, at, size):
+        total = turned[k % 2, :size, :].T
         for q, out in enumerate(outs):
             out[:, at : at + size] = total[q * rows : (q + 1) * rows, :].astype(out.dtype)
+
+    spans = pieces(width, 1024, 256)
+    for k, (copy, (at, size)) in enumerate(zip(copies, spans)):
+        copy.wait()
+        total = jnp.dot(
+            w_vmem[at : at + size, :depth], grads_t[:depth], preferred_element_type=F32
+        )
+        total += jnp.dot(
+            w_vmem[at : at + size, depth:], grads_t[depth:], preferred_element_type=F32
+        )
+        turned[k % 2, :size, :] = total
+        if k:
+            put(k - 1, *spans[k - 1])
+    put(len(spans) - 1, *spans[-1])
 
 
 def blocks_of(held, z, n_z):
@@ -106,22 +120,22 @@
 
 def first_half_kernel(n_t, n_z, offset, place, *refs):
     parts, w_hbm = refs[:n_t], refs[n_t]
-    grads_out, grads_t, *outs = refs[-5 - n_z : -3]
-    w_vmem, held, sems = refs[-3:]
+    grads_out, grads_t, *outs = refs[-6 - n_z : -4]
+    w_vmem, turned, held, sems = refs[-4:]
     width = outs[0].shape[1]
     copies = load_down((1 - place[0]) * offset, width, w_hbm, w_vmem, sems)
     hold(parts, 0, place[2], held)
     grads_t[...] = held[...].T.astype(BF16)
     grads_out[...] = blocks_of(held, place[1], n_z).astype(BF16)
-    hidden_half(copies, grads_t[...], width, w_vmem, outs)
-
-
-def second_half_kernel(offset, place, grads_t, w_hbm, *refs):
-    out, w_vmem, sems = refs[-3:]
+    hidden_half(copies, grads_t[...], width, w_vmem, outs, turned)
+
+
+def second_half_kernel(offset, base, place, grads_t, w_hbm, *refs):
+    out, w_vmem, turned, sems = refs[-4:]
     width = out.shape[2]
     outs = [out.at[q] for q in range(out.shape[0])]
-    copies = load_down(place[0] * offset, width, w_hbm, w_vmem, sems)
-    hidden_half(copies, grads_t[...], width, w_vmem, outs)
+    copies = load_down(place[0] * offset + base, width, w_hbm, w_vmem, sems)
+    hidden_half(copies, grads_t[...], width, w_vmem, outs, turned)
 
 
 def first_half(place, parts, w_down, n_z, width, *done):
@@ -139,6 +153,7 @@
         out_specs=(whole(),) * (2 + n_z),
         scratch_shapes=[
             VMEM((width, chans), BF16),
+            VMEM((2, min(width, 1024), tokens), F32),
             VMEM((tokens, chans), F32),
             pltpu.SemaphoreType.DMA((n_copies,)),
         ],
@@ -147,25 +162,29 @@
     )(place, *parts, w_down, *done)
 
 
-def second_half(place, grads_t, w_down, n_z, width, *done):
+def second_half(place, grads_t, w_down, n_z, offset, base, width, *done):
     chans, tokens = grads_t.shape
     n_copies = len(pieces(width, 1024, 256))
     return pl.pallas_call(
-        functools.partial(second_half_kernel, w_down.shape[0] - width),
+        functools.partial(second_half_kernel, offset, base),
         out_shape=shape((n_z, tokens // n_z, width), F32),
         in_specs=[whole(SMEM), whole(), whole(pltpu.HBM)] + after(done),
         out_specs=whole(),
-        scratch_shapes=[VMEM((width, chans), BF16), pltpu.SemaphoreType.DMA((n_copies,))],
+        scratch_shapes=[
+            VMEM((width, chans), BF16),
+            VMEM((2, min(width, 1024), tokens), F32),
+            pltpu.SemaphoreType.DMA((n_copies,)),
+        ],
         compiler_params=params(44),
         cost_estimate=cost(24 * tokens * chans * width, 24 * chans * width),
     )(place, grads_t, w_down, *done)
 
 
-def pair_kernel(place, mine, *refs):
-    n_z = mine.shape[0]
+def pair_kernel(base, place, mine, *refs):
+    n_z, _, width = mine.shape
     theirs, outs, total_ref = refs[:n_z], refs[-2 - n_z // 2 : -1], refs[-1]
     for q in range(n_z):
-        total_ref[q] = mine[q] + theirs[q][...].astype(F32)
+        total_ref[q] = mine[q] + theirs[q][:, base : base + width].astype(F32)
     for m in range(n_z):
         total = total_ref[place[1] ^ m]
         if m % 2:
@@ -174,10 +193,10 @@
             outs[m // 2][...] = total
 
 
-def pair_sum(place, mine, theirs, *done):
+def pair_sum(place, mine, theirs, base, *done):
     n_z, rows, width = mine.shape
     return pl.pallas_call(
-        pair_kernel,
+        functools.partial(pair_kernel, base),
         out_shape=(shape((rows, width), F32),) * (n_z // 2)
         + (shape((n_z // 2, rows, width), BF16),),
         in_specs=[whole(SMEM)] + [whole()] * (1 + n_z) + after(done),
@@ -188,34 +207,35 @@
     )(place, mine, *theirs, *done)
 
 
-def add_kernel(picks, n_refs, *refs):
-    outs = refs[-len(picks) :]
-    for pick, out in zip(picks, outs):
+def add_kernel(picks, *refs):
+    out = refs[-1]
+    for at, size, pick in picks:
         total = None
-        for ref, row in pick:
-            term = (refs[ref][...] if row is None else refs[ref][row]).astype(F32)
+        for ref, row, col in pick:
+            cols = slice(col, col + size)
+            term = (refs[ref][:, cols] if row is None else refs[ref][row, :, cols]).astype(F32)
             total = term if total is None else total + term
-        out[...] = total.astype(out.dtype)
-
-
-def add_all(lists, dtypes, done=()):
+        out[:, at : at + size] = total.astype(out.dtype)
+
+
+def add_all(spans, done):
     arrays, picks = [], []
-    for terms in lists:
+    for at, size, terms in spans:
         pick = []
-        for array, row in terms:
-            at = next((k for k, known in enumerate(arrays) if known is array), len(arrays))
-            if at == len(arrays):
+        for array, row, col in terms:
+            k = next((k for k, known in enumerate(arrays) if known is array), len(arrays))
+            if k == len(arrays):
                 arrays.append(array)
-            pick.append((at, row))
-        picks.append(pick)
-    dims = lists[0][0][0].shape[-2:]
-    return pl.pallas_call(
-        functools.partial(add_kernel, picks, len(arrays)),
-        out_shape=tuple(shape(dims, dtype) for dtype in dtypes),
+            pick.append((k, row, col))
+        picks.append((at, size, pick))
+    dims = (spans[0][2][0][0].shape[-2], sum(size for _, size, _ in spans))
+    return pl.pallas_call(
+        functools.partial(add_kernel, picks),
+        out_shape=shape(dims, BF16),
         in_specs=[whole()] * len(arrays) + after(done),
-        out_specs=(whole(),) * len(lists),
+        out_specs=whole(),
         compiler_params=params(6),
-        cost_estimate=cost(0, dims[0] * dims[1] * 6 * sum(map(len, lists))),
+        cost_estimate=cost(0, dims[0] * dims[1] * 6 * len(spans[0][2])),
     )(*arrays, *done)
 
 
@@ -255,16 +275,20 @@
     return [held[m] for m in range(n_z)]
 
 
-def reduce_z(evens, odds, n_z, done):
-    got = to_chip(odds, 1, n_z)
-    held = {2 * k: [(even, None), (got, k)] for k, even in enumerate(evens)}
+def reduce_z(spans, n_z, done):
+    held = {m: [] for m in range(0, n_z, 2)}
+    for at, size, evens, odds in spans:
+        got = to_chip(odds, 1, n_z)
+        for k, even in enumerate(evens):
+            held[2 * k].append((at, size, [(even, None, 0), (got, k, 0)]))
     bit = 2
     while bit < n_z:
         for m in [m for m in held if m & bit]:
-            (term,) = add_all([held.pop(m)], [BF16], done[0])
-            held[m ^ bit].append((to_chip(term, bit, n_z), None))
+            term = to_chip(add_all(held.pop(m), done[0]), bit, n_z)
+            for at, _, terms in held[m ^ bit]:
+                terms.append((term, None, at))
         bit *= 2
-    return add_all([held[0]], [BF16], done[1])[0]
+    return add_all(held[0], done[1])
 
 
 def gate_up_rows(core0, mine, theirs, cols):
@@ -404,7 +428,7 @@
             VMEM((tokens, chans), F32),
             pltpu.SemaphoreType.DMA((2, slots)),
         ],
-        compiler_params=params(42),
+        compiler_params=params(38),
         cost_estimate=cost(4 * tokens * chans * ff, 4 * chans * ff + 12 * tokens * ff),
     )(place, *hidden[0], *hidden[1], *gate_up[0], *gate_up[1], w_gate, w_up)
 
@@ -466,16 +490,18 @@
     rows = {0: rows, bit: to_chip(rows, bit, n_z), 1: to_chip(rows, 1, n_z)}
     grads, grads_t, *send = first_half(place, both, w_down, n_z, width)
     got = [to_core(part) for part in send]
-    mine = second_half(place, grads_t, w_down, n_z, width, rows[1], rows[bit])
+    mine = second_half(place, grads_t, w_down, n_z, ff - width, 0, width, rows[1], rows[bit])
     rows[bit | 1] = to_chip(rows[bit], 1, n_z)
-    *evens, odds = pair_sum(place, mine, got, rows[bit | 1])
+    *evens, odds = pair_sum(place, mine, got, 0)
+    spans = [(0, width, evens, odds)]
     rows = complete_z(rows, n_z)
     gate_up = (rows, [to_core(part) for part in rows])
     grad_down, token = down_grad(place, *gate_up, grads, 0, ff - width)
-    hidden = {0: reduce_z(evens, odds, n_z, (gate_up[1], [token]))}
+    early = [part for m, part in enumerate(gate_up[1]) if m != bit | 1]
+    hidden = {0: reduce_z(spans, n_z, (early, [token]))}
     hidden |= {bit: to_chip(hidden[0], bit, n_z), 1: to_chip(hidden[0], 1, n_z)}
     grad_down, token = down_grad(place, *gate_up, grads, ff - width, width, grad_down)
-    (hidden[bit],) = add_all([[(hidden[bit], None)]], [BF16], [token, hidden[1]])
+    hidden[bit] = add_all([(0, width, [(hidden[bit], None, 0)])], [token, hidden[1]])
     hidden = complete_z(hidden, n_z)
     gate_grad, up_grad, sends = input_grad(
         place, (hidden, [to_core(part) for part in hidden]), gate_up, w_gate, w_up, n_t

time: 104 us -> 99.8 us (0.960)
  waiting for transfers between devices: 31.5 us -> 25.8 us
  starting transfers between devices: 18.7 us -> 20.5 us
    ppermute x8, waiting for transfers between devices: 25.6 us -> 20.2 us  [to_chip(): return lax.ppermute(value, 'z', [(a, a ^ bit) for a in range(n_z)])]
    ppermute x8, starting transfers between devices: 9.26 us -> 11.1 us  [to_chip(): return lax.ppermute(value, 'z', [(a, a ^ bit) for a in range(n_z)])]
  transfers between devices with their start and end apart: 24 -> 24, of which waited for: 11 -> 10; matrix products, arithmetic and copies ran while one was open for 0% -> 0% of each run, Pallas kernels for 31% -> 32%
where the time goes in v1:
time: 99.8 us; the launch traced here: 99.5 us
  Pallas kernels  49 us (49%)
  waiting for transfers between devices  25.8 us (26%)
  starting transfers between devices  20.5 us (21%)
  local copies, waits for them, and re-layouts  3.24 us (3%)
    ppermute x8, waiting for transfers between devices, to_chip(): return lax.ppermute(value, 'z', [(a, a ^ bit) for a in range(n_z)])  20.2 us
    pallas_call x1, Pallas kernels, input_grad(): pl.pallas_call(functools.partial(input_kernel, n_z), out_shape=(shape((to...  14.5 us
    pallas_call x1, Pallas kernels, weight_grads(): pl.pallas_call(functools.partial(weight_kernel, n_z, n_t), out_shape=(sha...  11.5 us
    ppermute x8, starting transfers between devices, to_chip(): return lax.ppermute(value, 'z', [(a, a ^ bit) for a in range(n_z)])  11.1 us
    pallas_call x2, Pallas kernels, down_grad(): pl.pallas_call(functools.partial(down_kernel, base, ff, n_z), out_shape=(...  8.31 us
    pallas_call x1, Pallas kernels, second_half(): pl.pallas_call(functools.partial(second_half_kernel, offset, base), out_s...  5.68 us
    pallas_call x1, Pallas kernels, first_half(): pl.pallas_call(functools.partial(first_half_kernel, n_t, n_z, w_down.shap...  5.66 us
    ppermute x3, waiting for transfers between devices, from_tensor(): lax.ppermute(own, 'tensor', [(a, a ^ s) for a in range(n_t)])  4.21 us
  transfers between devices with their start and end apart: 24, of which 10 were waited for; matrix products, arithmetic and copies ran while one was open for 0% of the time, Pallas kernels for 32%

profile of v1, /device:TPU:0, one launch (start us, length us, event | category | flops | bytes accessed | tf_op | source)
XLA Modules:
  0.0 99.5 jit_solution(4332961276387878331)
XLA Ops:
  0.6 2.0 %shard_map.156 = (bf16[2,24,1024]{2,1,0:T(8,128)(2,1)}, bf16[24,6656]{1,0:T(8,128)(2,1)}) custom-call(bf16[24,1024]{1,0:T(8,128)(2,1)} %xq.1, f32[1,8]{1,0:T(1,128)} %xs.1, s32[1,8]{1,0:T(1,128)} %xo.1, bf16[24,1024]{1,0:T(8,128)(2,1)} %xc.1, bf16[24,1024]{1,0:T(8,128)(2,1)} %gq.1, f32[1,8]{1,0:T(1,128)} %gs.1, s32[1,8]{1,0:T(1,128)} %go.1, ...), custom_call_target="tpu_custom_call" | custom-call | bytes 835584 | tf_op jit(solution)/shard_map/pallas_call | solution.py:58
  2.6 4.0 %collective-permute-start.4 = (bf16[24,6656]{1,0:T(8,128)(2,1)}, bf16[24,6656]{1,0:T(8,128)(2,1)S(1)}, u32[]{:S(2)}, u32[]{:S(2)}) collective-permute-start(bf16[24,6656]{1,0:T(8,128)(2,1)} %get-tuple-element.26.refs_0_.refs_8_), channel_id=1, source_target_pairs={{0,16},{8,24},{16,0},{24,8},{1,17},{9,25},{17,1},{25,9},{2,18},{10... | collective-permute-start | bytes 958472 | tf_op jit(solution)/shard_map/ppermute | solution.py:261
  6.7 1.6 %collective-permute-start.3 = (bf16[24,6656]{1,0:T(8,128)(2,1)}, bf16[24,6656]{1,0:T(8,128)(2,1)S(1)}, u32[]{:S(2)}, u32[]{:S(2)}) collective-permute-start(bf16[24,6656]{1,0:T(8,128)(2,1)} %get-tuple-element.26.refs_0_.refs_8_), channel_id=1, source_target_pairs={{0,8},{8,0},{16,24},{24,16},{1,9},{9,1},{17,25},{25,17},{2,10},{10... | collective-permute-start | bytes 958472 | tf_op jit(solution)/shard_map/ppermute | solution.py:261
  8.2 2.4 %collective-permute-start.2 = (bf16[2,24,1024]{2,1,0:T(8,128)(2,1)}, bf16[2,24,1024]{2,1,0:T(8,128)(2,1)S(1)}, u32[]{:S(2)}, u32[]{:S(2)}) collective-permute-start(bf16[2,24,1024]{2,1,0:T(8,128)(2,1)} %get-tuple-element.24.refs_0_), channel_id=1, source_target_pairs={{0,3},{1,2},{2,1},{3,0},{4,7},{5,6},{6,5},{7,4},{8,11},{9,10},{10,... | collective-permute-start | bytes 294920 | tf_op jit(solution)/shard_map/ppermute | solution.py:484
  11.8 2.5 %collective-permute-done.2.refs_3_ = bf16[2,24,1024]{2,1,0:T(8,128)(2,1)S(1)} collective-permute-done((bf16[2,24,1024]{2,1,0:T(8,128)(2,1)}, bf16[2,24,1024]{2,1,0:T(8,128)(2,1)S(1)}, u32[]{:S(2)}, u32[]{:S(2)}) %collective-permute-start.2) | collective-permute-done | bytes 98336 | tf_op jit(solution)/shard_map/ppermute | solution.py:484
  14.3 1.3 %collective-permute-done.1.refs_2_ = bf16[2,24,1024]{2,1,0:T(8,128)(2,1)S(1)} collective-permute-done((bf16[2,24,1024]{2,1,0:T(8,128)(2,1)}, bf16[2,24,1024]{2,1,0:T(8,128)(2,1)S(1)}, u32[]{:S(2)}, u32[]{:S(2)}) %collective-permute-start.1) | collective-permute-done | bytes 98336 | tf_op jit(solution)/shard_map/ppermute | solution.py:484
  16.0 0.9 copy-done.1
  16.9 5.7 %shard_map.157 = (bf16[96,1024]{1,0:T(8,128)(2,1)S(1)}, bf16[1024,96]{1,0:T(8,128)(2,1)S(1)}, bf16[24,3328]{1,0:T(8,128)(2,1)S(1)}, bf16[24,3328]{1,0:T(8,128)(2...) custom-call(s32[3]{0:T(128)S(1)} %pad_add_fusion.place, bf16[2,24,1024]{2,1,0:T(8,128)(2,1)S(1)} %copy-done.1, ...), custom_call_target="tpu_custom_call" | custom-call | flops 654311424 | bytes 6815744 | tf_op jit(solution)/shard_map/pallas_call | solution.py:145
  24.1 5.7 %shard_map.158.mine = f32[4,24,3328]{2,1,0:T(8,128)S(1)} custom-call(s32[3]{0:T(128)S(1)} %pad_add_fusion.place, bf16[1024,96]{1,0:T(8,128)(2,1)S(1)} %get-tuple-element.25.grads_t, bf16[6656,1024]{1,0:T(8,128)(2,1)} %w_hbm.1, bf16[24,6656]{1,0:T(8,128)(2,1)S(1)} %collective-permute-done.3.refs_0_.refs_1_.refs_9_, ...), custom_call_target="tpu_custom_call" | custom-call | flops 7851737088 | bytes 81788928 | tf_op jit(solution)/shard_map/pallas_call | solution.py:168
  31.2 1.6 %collective-permute-start.9 = (bf16[2,24,3328]{2,1,0:T(8,128)(2,1)S(1)}, bf16[2,24,3328]{2,1,0:T(8,128)(2,1)S(1)}, u32[]{:S(2)}, u32[]{:S(2)}) collective-permute-start(bf16[2,24,3328]{2,1,0:T(8,128)(2,1)S(1)} %get-tuple-element.32), channel_id=1, source_target_pairs={{0,8},{8,0},{16,24},{24,16},{1,9},{9,1},{17,25},{25,17},{2,10},{10... | collective-permute-start | bytes 958472 | tf_op jit(solution)/shard_map/ppermute | solution.py:261
  33.2 8.0 %collective-permute-done.9.refs_1_ = bf16[2,24,3328]{2,1,0:T(8,128)(2,1)S(1)} collective-permute-done((bf16[2,24,3328]{2,1,0:T(8,128)(2,1)S(1)}, bf16[2,24,3328]{2,1,0:T(8,128)(2,1)S(1)}, u32[]{:S(2)}, u32[]{:S(2)}) %collective-permute-start.9) | collective-permute-done | bytes 319520 | tf_op jit(solution)/shard_map/ppermute | solution.py:261
  41.2 1.3 %collective-permute-start.13 = (bf16[24,3328]{1,0:T(8,128)(2,1)S(1)}, bf16[24,3328]{1,0:T(8,128)(2,1)S(1)}, u32[]{:S(2)}, u32[]{:S(2)}) collective-permute-start(bf16[24,3328]{1,0:T(8,128)(2,1)S(1)} %shard_map.160), channel_id=1, source_target_pairs={{0,16},{8,24},{16,0},{24,8},{1,17},{9,25},{17,1},{25,9},{2,18},{10... | collective-permute-start | bytes 479240 | tf_op jit(solution)/shard_map/ppermute | solution.py:261
  42.5 4.2 %shard_map.161 = (bf16[6656,1024]{1,0:T(8,128)(2,1)}, f32[8,128]{1,0:T(8,128)S(1)}) custom-call(s32[3]{0:T(128)S(1)} %pad_add_fusion.place, bf16[24,6656]{1,0:T(8,128)(2,1)S(1)} %copy-done, bf16[24,6656]{1,0:T(8,128)(2,1)S(1)} %collective-permute-done.3.refs_0_.refs_1_.refs_9_, bf16[24,6656]{1,0:T(8,128)(2,1)S(1)} %collective-permute-done.4.refs_1_.refs_2_.refs_10_, ...), custom_call_target="tpu_custom_call" | custom-call | flops 654311424 | bytes 6815744 | tf_op jit(solution)/shard_map/pallas_call | solution.py:331
  46.7 4.6 %collective-permute-done.13.refs_2_ = bf16[24,3328]{1,0:T(8,128)(2,1)S(1)} collective-permute-done((bf16[24,3328]{1,0:T(8,128)(2,1)S(1)}, bf16[24,3328]{1,0:T(8,128)(2,1)S(1)}, u32[]{:S(2)}, u32[]{:S(2)}) %collective-permute-start.13) | collective-permute-done | bytes 159776 | tf_op jit(solution)/shard_map/ppermute | solution.py:261
  51.4 1.9 %collective-permute-start.16 = (bf16[24,3328]{1,0:T(8,128)(2,1)S(1)}, bf16[24,3328]{1,0:T(8,128)(2,1)S(1)}, u32[]{:S(2)}, u32[]{:S(2)}) collective-permute-start(bf16[24,3328]{1,0:T(8,128)(2,1)S(1)} %shard_map.162.refs_0_), channel_id=1, source_target_pairs={{0,8},{8,0},{16,24},{24,16},{1,9},{9,1},{17,25},{25,17},{2,10},{10... | collective-permute-start | bytes 479240 | tf_op jit(solution)/shard_map/ppermute | solution.py:261
  53.3 4.2 %shard_map.163 = (bf16[6656,1024]{1,0:T(8,128)(2,1)}, f32[8,128]{1,0:T(8,128)S(1)}) custom-call(s32[3]{0:T(128)S(1)} %pad_add_fusion.place, bf16[24,6656]{1,0:T(8,128)(2,1)S(1)} %copy-done, bf16[24,6656]{1,0:T(8,128)(2,1)S(1)} %collective-permute-done.3.refs_0_.refs_1_.refs_9_, ...), custom_call_target="tpu_custom_call", output_to_operand_aliasing={{0}: (10, {})} | custom-call | flops 654311424 | bytes 6815744 | tf_op jit(solution)/shard_map/pallas_call | solution.py:331
  57.5 2.4 %collective-permute-done.17.refs_0_ = bf16[24,3328]{1,0:T(8,128)(2,1)S(1)} collective-permute-done((bf16[24,3328]{1,0:T(8,128)(2,1)S(1)}, bf16[24,3328]{1,0:T(8,128)(2,1)S(1)}, u32[]{:S(2)}, u32[]{:S(2)}) %collective-permute-start.17) | collective-permute-done | bytes 159776 | tf_op jit(solution)/shard_map/ppermute | solution.py:261
  60.8 4.7 %collective-permute-done.18.refs_3_ = bf16[24,3328]{1,0:T(8,128)(2,1)S(1)} collective-permute-done((bf16[24,3328]{1,0:T(8,128)(2,1)S(1)}, bf16[24,3328]{1,0:T(8,128)(2,1)S(1)}, u32[]{:S(2)}, u32[]{:S(2)}) %collective-permute-start.18) | collective-permute-done | bytes 159776 | tf_op jit(solution)/shard_map/ppermute | solution.py:261
  65.6 1.4 %collective-permute-done.22.refs_7_ = bf16[24,3328]{1,0:T(8,128)(2,1)S(1)} collective-permute-done((bf16[24,3328]{1,0:T(8,128)(2,1)S(1)}, bf16[24,3328]{1,0:T(8,128)(2,1)S(1)}, u32[]{:S(2)}, u32[]{:S(2)}) %collective-permute-start.22) | collective-permute-done | bytes 159776 | tf_op jit(solution)/shard_map/ppermute | solution.py:265
  67.0 14.5 %shard_map.165 = (bf16[96,6656]{1,0:T(8,128)(2,1)S(1)}, bf16[96,6656]{1,0:T(8,128)(2,1)S(1)}, bf16[4,24,1024]{2,1,0:T(8,128)(2,1)}) custom-call(s32[3]{0:T(128)S(1)} %pad_add_fusion.place, bf16[24,3328]{1,0:T(8,128)(2,1)S(1)} %shard_map.162.refs_0_, bf16[24,3328]{1,0:T(8,128)(2,1)S(1)} %collective-permute-done.16.refs_2_.refs_1_, ...), custom_call_target="tpu_custom_call" | custom-call | flops 2617245696 | bytes 34930688 | tf_op jit(solution)/shard_map/pallas_call | solution.py:419
  81.4 1.0 %copy-done.3 = bf16[96,6656]{1,0:T(8,128)(2,1)} copy-done((bf16[96,6656]{1,0:T(8,128)(2,1)}, bf16[96,6656]{1,0:T(8,128)(2,1)S(1)}, u32[]{:S(2)}) %copy-start.3) | copy-done | bytes 1277976
  82.5 3.6 %all-to-all-start = ((bf16[4,24,1024]{2,1,0:T(8,128)(2,1)}), bf16[4,24,1024]{2,1,0:T(8,128)(2,1)S(1)}, u32[]{:S(2)}, u32[]{:S(2)}) async-start(bf16[4,24,1024]{2,1,0:T(8,128)(2,1)} %get-tuple-element.38), calls=%async_computation | async-start | bytes 393216 | tf_op jit(solution)/shard_map/all_to_all | solution.py:509
  86.1 1.3 %copy-done.4 = bf16[96,6656]{1,0:T(8,128)(2,1)S(1)} copy-done((bf16[96,6656]{1,0:T(8,128)(2,1)S(1)}, bf16[96,6656]{1,0:T(8,128)(2,1)}, u32[]{:S(2)}) %copy-start.4) | copy-done | bytes 1277976
  87.4 11.5 %shard_map.167 = (bf16[1024,6656]{1,0:T(8,128)(2,1)}, bf16[1024,6656]{1,0:T(8,128)(2,1)}) custom-call(s32[3]{0:T(128)S(1)} %pad_add_fusion.place, bf16[2,24,1024]{2,1,0:T(8,128)(2,1)S(1)} %copy-done.2, bf16[2,24,1024]{2,1,0:T(8,128)(2,1)S(1)} %collective-permute-done.refs_1_, bf16[2,24,1024]{2,1,0:T(8,128)(2,1)S(1)} %collective-permute-done.1.refs_2_, ...), custom_call_target="tpu_custom_call" | custom-call | flops 2617245696 | bytes 29818880 | tf_op jit(solution)/shard_map/pallas_call | solution.py:461
  (47 shorter events, 6.5 us)
Async XLA Ops:
  2.6 20.6 %collective-permute-start.4 = (bf16[24,6656]{1,0:T(8,128)(2,1)}, bf16[24,6656]{1,0:T(8,128)(2,1)S(1)}, u32[]{:S(2)}, u32[]{:S(2)}) collective-permute-start(bf16[24,6656]{1,0:T(8,128)(2,1)} %get-tuple-element.26.refs_0_.refs_8_), channel_id=1, source_target_pairs={{0,16},{8,24},{16,0},{24,8},{1,17},{9,25},{17,1},{25,9},{2,18},{10... | collective-permute-start | bytes 958472 | tf_op jit(solution)/shard_map/ppermute | solution.py:261
  6.7 17.0 %collective-permute-start.3 = (bf16[24,6656]{1,0:T(8,128)(2,1)}, bf16[24,6656]{1,0:T(8,128)(2,1)S(1)}, u32[]{:S(2)}, u32[]{:S(2)}) collective-permute-start(bf16[24,6656]{1,0:T(8,128)(2,1)} %get-tuple-element.26.refs_0_.refs_8_), channel_id=1, source_target_pairs={{0,8},{8,0},{16,24},{24,16},{1,9},{9,1},{17,25},{25,17},{2,10},{10... | collective-permute-start | bytes 958472 | tf_op jit(solution)/shard_map/ppermute | solution.py:261
  8.2 6.1 %collective-permute-start.2 = (bf16[2,24,1024]{2,1,0:T(8,128)(2,1)}, bf16[2,24,1024]{2,1,0:T(8,128)(2,1)S(1)}, u32[]{:S(2)}, u32[]{:S(2)}) collective-permute-start(bf16[2,24,1024]{2,1,0:T(8,128)(2,1)} %get-tuple-element.24.refs_0_), channel_id=1, source_target_pairs={{0,3},{1,2},{2,1},{3,0},{4,7},{5,6},{6,5},{7,4},{8,11},{9,10},{10,... | collective-permute-start | bytes 294920 | tf_op jit(solution)/shard_map/ppermute | solution.py:484
  10.7 5.0 %collective-permute-start.1 = (bf16[2,24,1024]{2,1,0:T(8,128)(2,1)}, bf16[2,24,1024]{2,1,0:T(8,128)(2,1)S(1)}, u32[]{:S(2)}, u32[]{:S(2)}) collective-permute-start(bf16[2,24,1024]{2,1,0:T(8,128)(2,1)} %get-tuple-element.24.refs_0_), channel_id=1, source_target_pairs={{0,2},{1,3},{2,0},{3,1},{4,6},{5,7},{6,4},{7,5},{8,10},{9,11},{10,... | collective-permute-start | bytes 294920 | tf_op jit(solution)/shard_map/ppermute | solution.py:484
  11.2 4.8 %collective-permute-start = (bf16[2,24,1024]{2,1,0:T(8,128)(2,1)}, bf16[2,24,1024]{2,1,0:T(8,128)(2,1)S(1)}, u32[]{:S(2)}, u32[]{:S(2)}) collective-permute-start(bf16[2,24,1024]{2,1,0:T(8,128)(2,1)} %get-tuple-element.24.refs_0_), channel_id=1, source_target_pairs={{0,1},{1,0},{2,3},{3,2},{4,5},{5,4},{6,7},{7,6},{8,9},{9,8},{10,11... | collective-permute-start | bytes 294920 | tf_op jit(solution)/shard_map/ppermute | solution.py:484
  22.6 7.2 %collective-permute-start.5 = (bf16[24,3328]{1,0:T(8,128)(2,1)S(1)}, bf16[24,3328]{1,0:T(8,128)(2,1)S(1)}, u32[]{:S(2)}, u32[]{:S(2)}) collective-permute-start(bf16[24,3328]{1,0:T(8,128)(2,1)S(1)} %get-tuple-element.27), channel_id=1, source_target_pairs={{0,4},{4,0},{1,5},{5,1},{2,6},{6,2},{3,7},{7,3},{8,12},{12,8},{9,1... | collective-permute-start | bytes 479240 | tf_op jit(solution)/shard_map/ppermute | solution.py:265
  22.6 7.3 %collective-permute-start.6 = (bf16[24,3328]{1,0:T(8,128)(2,1)S(1)}, bf16[24,3328]{1,0:T(8,128)(2,1)S(1)}, u32[]{:S(2)}, u32[]{:S(2)}) collective-permute-start(bf16[24,3328]{1,0:T(8,128)(2,1)S(1)} %get-tuple-element.28), channel_id=1, source_target_pairs={{0,4},{4,0},{1,5},{5,1},{2,6},{6,2},{3,7},{7,3},{8,12},{12,8},{9,1... | collective-permute-start | bytes 479240 | tf_op jit(solution)/shard_map/ppermute | solution.py:265
  23.1 7.3 %collective-permute-start.7 = (bf16[24,3328]{1,0:T(8,128)(2,1)S(1)}, bf16[24,3328]{1,0:T(8,128)(2,1)S(1)}, u32[]{:S(2)}, u32[]{:S(2)}) collective-permute-start(bf16[24,3328]{1,0:T(8,128)(2,1)S(1)} %get-tuple-element.29), channel_id=1, source_target_pairs={{0,4},{4,0},{1,5},{5,1},{2,6},{6,2},{3,7},{7,3},{8,12},{12,8},{9,1... | collective-permute-start | bytes 479240 | tf_op jit(solution)/shard_map/ppermute | solution.py:265
  23.2 7.3 %collective-permute-start.8 = (bf16[24,3328]{1,0:T(8,128)(2,1)S(1)}, bf16[24,3328]{1,0:T(8,128)(2,1)S(1)}, u32[]{:S(2)}, u32[]{:S(2)}) collective-permute-start(bf16[24,3328]{1,0:T(8,128)(2,1)S(1)} %get-tuple-element.30), channel_id=1, source_target_pairs={{0,4},{4,0},{1,5},{5,1},{2,6},{6,2},{3,7},{7,3},{8,12},{12,8},{9,1... | collective-permute-start | bytes 479240 | tf_op jit(solution)/shard_map/ppermute | solution.py:265
  23.7 9.5 %collective-permute-start.14 = (bf16[24,6656]{1,0:T(8,128)(2,1)S(1)}, bf16[24,6656]{1,0:T(8,128)(2,1)S(1)}, u32[]{:S(2)}, u32[]{:S(2)}) collective-permute-start(bf16[24,6656]{1,0:T(8,128)(2,1)S(1)} %collective-permute-done.4.refs_1_.refs_2_.refs_10_), channel_id=1, source_target_pairs={{0,8},{8,0},{16,24},{24,16},{1,9},{9,1},{17,25},{25,17},{2,10},{10... | collective-permute-start | bytes 958472 | tf_op jit(solution)/shard_map/ppermute | solution.py:261
  29.8 3.4 %collective-permute-start.10 = (bf16[24,6656]{1,0:T(8,128)(2,1)S(1)}, bf16[24,6656]{1,0:T(8,128)(2,1)S(1)}, u32[]{:S(2)}, u32[]{:S(2)}) collective-permute-start(bf16[24,6656]{1,0:T(8,128)(2,1)S(1)} %copy-done), channel_id=1, source_target_pairs={{0,4},{4,0},{1,5},{5,1},{2,6},{6,2},{3,7},{7,3},{8,12},{12,8},{9,1... | collective-permute-start | bytes 958472 | tf_op jit(solution)/shard_map/ppermute | solution.py:265
  29.9 3.3 %collective-permute-start.12 = (bf16[24,6656]{1,0:T(8,128)(2,1)S(1)}, bf16[24,6656]{1,0:T(8,128)(2,1)S(1)}, u32[]{:S(2)}, u32[]{:S(2)}) collective-permute-start(bf16[24,6656]{1,0:T(8,128)(2,1)S(1)} %collective-permute-done.4.refs_1_.refs_2_.refs_10_), channel_id=1, source_target_pairs={{0,4},{4,0},{1,5},{5,1},{2,6},{6,2},{3,7},{7,3},{8,12},{12,8},{9,1... | collective-permute-start | bytes 958472 | tf_op jit(solution)/shard_map/ppermute | solution.py:265
  30.4 2.8 %collective-permute-start.11 = (bf16[24,6656]{1,0:T(8,128)(2,1)S(1)}, bf16[24,6656]{1,0:T(8,128)(2,1)S(1)}, u32[]{:S(2)}, u32[]{:S(2)}) collective-permute-start(bf16[24,6656]{1,0:T(8,128)(2,1)S(1)} %collective-permute-done.3.refs_0_.refs_1_.refs_9_), channel_id=1, source_target_pairs={{0,4},{4,0},{1,5},{5,1},{2,6},{6,2},{3,7},{7,3},{8,12},{12,8},{9,1... | collective-permute-start | bytes 958472 | tf_op jit(solution)/shard_map/ppermute | solution.py:265
  31.2 9.9 %collective-permute-start.9 = (bf16[2,24,3328]{2,1,0:T(8,128)(2,1)S(1)}, bf16[2,24,3328]{2,1,0:T(8,128)(2,1)S(1)}, u32[]{:S(2)}, u32[]{:S(2)}) collective-permute-start(bf16[2,24,3328]{2,1,0:T(8,128)(2,1)S(1)} %get-tuple-element.32), channel_id=1, source_target_pairs={{0,8},{8,0},{16,24},{24,16},{1,9},{9,1},{17,25},{25,17},{2,10},{10... | collective-permute-start | bytes 958472 | tf_op jit(solution)/shard_map/ppermute | solution.py:261
  33.2 9.3 %collective-permute-start.15 = (bf16[24,6656]{1,0:T(8,128)(2,1)S(1)}, bf16[24,6656]{1,0:T(8,128)(2,1)S(1)}, u32[]{:S(2)}, u32[]{:S(2)}) collective-permute-start(bf16[24,6656]{1,0:T(8,128)(2,1)S(1)} %collective-permute-done.14.refs_3_.refs_11_), channel_id=1, source_target_pairs={{0,4},{4,0},{1,5},{5,1},{2,6},{6,2},{3,7},{7,3},{8,12},{12,8},{9,1... | collective-permute-start | bytes 958472 | tf_op jit(solution)/shard_map/ppermute | solution.py:265
  41.2 10.1 %collective-permute-start.13 = (bf16[24,3328]{1,0:T(8,128)(2,1)S(1)}, bf16[24,3328]{1,0:T(8,128)(2,1)S(1)}, u32[]{:S(2)}, u32[]{:S(2)}) collective-permute-start(bf16[24,3328]{1,0:T(8,128)(2,1)S(1)} %shard_map.160), channel_id=1, source_target_pairs={{0,16},{8,24},{16,0},{24,8},{1,17},{9,25},{17,1},{25,9},{2,18},{10... | collective-permute-start | bytes 479240 | tf_op jit(solution)/shard_map/ppermute | solution.py:261
  51.3 8.6 %collective-permute-start.17 = (bf16[24,3328]{1,0:T(8,128)(2,1)S(1)}, bf16[24,3328]{1,0:T(8,128)(2,1)S(1)}, u32[]{:S(2)}, u32[]{:S(2)}) collective-permute-start(bf16[24,3328]{1,0:T(8,128)(2,1)S(1)} %shard_map.162.refs_0_), channel_id=1, source_target_pairs={{0,16},{8,24},{16,0},{24,8},{1,17},{9,25},{17,1},{25,9},{2,18},{10... | collective-permute-start | bytes 479240 | tf_op jit(solution)/shard_map/ppermute | solution.py:261
  51.4 8.7 %collective-permute-start.16 = (bf16[24,3328]{1,0:T(8,128)(2,1)S(1)}, bf16[24,3328]{1,0:T(8,128)(2,1)S(1)}, u32[]{:S(2)}, u32[]{:S(2)}) collective-permute-start(bf16[24,3328]{1,0:T(8,128)(2,1)S(1)} %shard_map.162.refs_0_), channel_id=1, source_target_pairs={{0,8},{8,0},{16,24},{24,16},{1,9},{9,1},{17,25},{25,17},{2,10},{10... | collective-permute-start | bytes 479240 | tf_op jit(solution)/shard_map/ppermute | solution.py:261
  60.1 5.5 %collective-permute-start.18 = (bf16[24,3328]{1,0:T(8,128)(2,1)S(1)}, bf16[24,3328]{1,0:T(8,128)(2,1)S(1)}, u32[]{:S(2)}, u32[]{:S(2)}) collective-permute-start(bf16[24,3328]{1,0:T(8,128)(2,1)S(1)} %shard_map.164.refs_2_), channel_id=1, source_target_pairs={{0,8},{8,0},{16,24},{24,16},{1,9},{9,1},{17,25},{25,17},{2,10},{10... | collective-permute-start | bytes 479240 | tf_op jit(solution)/shard_map/ppermute | solution.py:261
  60.2 5.4 %collective-permute-start.19 = (bf16[24,3328]{1,0:T(8,128)(2,1)S(1)}, bf16[24,3328]{1,0:T(8,128)(2,1)S(1)}, u32[]{:S(2)}, u32[]{:S(2)}) collective-permute-start(bf16[24,3328]{1,0:T(8,128)(2,1)S(1)} %shard_map.162.refs_0_), channel_id=1, source_target_pairs={{0,4},{4,0},{1,5},{5,1},{2,6},{6,2},{3,7},{7,3},{8,12},{12,8},{9,1... | collective-permute-start | bytes 479240 | tf_op jit(solution)/shard_map/ppermute | solution.py:265
  60.3 5.3 %collective-permute-start.21 = (bf16[24,3328]{1,0:T(8,128)(2,1)S(1)}, bf16[24,3328]{1,0:T(8,128)(2,1)S(1)}, u32[]{:S(2)}, u32[]{:S(2)}) collective-permute-start(bf16[24,3328]{1,0:T(8,128)(2,1)S(1)} %shard_map.164.refs_2_), channel_id=1, source_target_pairs={{0,4},{4,0},{1,5},{5,1},{2,6},{6,2},{3,7},{7,3},{8,12},{12,8},{9,1... | collective-permute-start | bytes 479240 | tf_op jit(solution)/shard_map/ppermute | solution.py:265
  60.8 4.8 %collective-permute-start.20 = (bf16[24,3328]{1,0:T(8,128)(2,1)S(1)}, bf16[24,3328]{1,0:T(8,128)(2,1)S(1)}, u32[]{:S(2)}, u32[]{:S(2)}) collective-permute-start(bf16[24,3328]{1,0:T(8,128)(2,1)S(1)} %collective-permute-done.16.refs_2_.refs_1_), channel_id=1, source_target_pairs={{0,4},{4,0},{1,5},{5,1},{2,6},{6,2},{3,7},{7,3},{8,12},{12,8},{9,1... | collective-permute-start | bytes 479240 | tf_op jit(solution)/shard_map/ppermute | solution.py:265
  65.6 1.4 %collective-permute-start.22 = (bf16[24,3328]{1,0:T(8,128)(2,1)S(1)}, bf16[24,3328]{1,0:T(8,128)(2,1)S(1)}, u32[]{:S(2)}, u32[]{:S(2)}) collective-permute-start(bf16[24,3328]{1,0:T(8,128)(2,1)S(1)} %collective-permute-done.18.refs_3_), channel_id=1, source_target_pairs={{0,4},{4,0},{1,5},{5,1},{2,6},{6,2},{3,7},{7,3},{8,12},{12,8},{9,1... | collective-permute-start | bytes 479240 | tf_op jit(solution)/shard_map/ppermute | solution.py:265
  82.5 16.4 %all-to-all-start = ((bf16[4,24,1024]{2,1,0:T(8,128)(2,1)}), bf16[4,24,1024]{2,1,0:T(8,128)(2,1)S(1)}, u32[]{:S(2)}, u32[]{:S(2)}) async-start(bf16[4,24,1024]{2,1,0:T(8,128)(2,1)} %get-tuple-element.38), calls=%async_computation | async-start | bytes 393216 | tf_op jit(solution)/shard_map/all_to_all | solution.py:509
  (5 other events, 34.9 us)

commit v2 on v1

--- a/solution.py
+++ b/solution.py
@@ -237,24 +237,6 @@
         compiler_params=params(6),
         cost_estimate=cost(0, dims[0] * dims[1] * 6 * len(spans[0][2])),
     )(*arrays, *done)
-
-
-def sum_kernel(parts, out):
-    total = parts[0].astype(F32)
-    for p in range(1, parts.shape[0]):
-        total = total + parts[p].astype(F32)
-    out[...] = total.astype(BF16)
-
-
-def sum_parts(parts):
-    return pl.pallas_call(
-        sum_kernel,
-        out_shape=shape(parts.shape[1:], BF16),
-        in_specs=[whole()],
-        out_specs=whole(),
-        compiler_params=params(3),
-        cost_estimate=cost(0, parts.size * 3),
-    )(parts)
 
 
 def to_chip(value, bit, n_z):
@@ -345,7 +327,8 @@
         (refs[2 * k * n_z : (2 * k + 1) * n_z], refs[(2 * k + 1) * n_z : (2 * k + 2) * n_z])
         for k in range(2)
     ]
-    gate_hbm, up_hbm, gate_grad, up_grad, out, w_gate, w_up, total, held, sems = refs[4 * n_z :]
+    gate_hbm, up_hbm, gate_grad, up_grad, *outs = refs[4 * n_z : -5]
+    w_gate, w_up, total, held, sems = refs[-5:]
     core0, z = place[0] == 0, place[1]
     rows, width = hidden[0][0].shape
     ff = gate_grad.shape[1]
@@ -406,10 +389,10 @@
     for m in range(n_z):
         start = pl.multiple_of((z ^ m) * rows, math.gcd(rows, 8))
         held[pl.ds(start, rows), :] = turned[m * rows : (m + 1) * rows]
-    n_t = out.shape[0]
-    step = held.shape[0] // n_t
-    for p in range(n_t):
-        out[p] = held[p * step : (p + 1) * step, :].astype(BF16)
+    for s, out in enumerate(outs):
+        step = out.shape[0]
+        start = pl.multiple_of((place[2] ^ s) * step, math.gcd(step, 8))
+        out[...] = held[pl.ds(start, step), :].astype(out.dtype)
 
 
 def input_grad(place, hidden, gate_up, w_gate, w_up, n_t):
@@ -418,9 +401,11 @@
     chans, ff = w_gate.shape
     return pl.pallas_call(
         functools.partial(input_kernel, n_z),
-        out_shape=(shape((tokens, ff), BF16),) * 2 + (shape((n_t, tokens // n_t, chans), BF16),),
+        out_shape=(shape((tokens, ff), BF16),) * 2
+        + (shape((tokens // n_t, chans), F32),)
+        + (shape((tokens // n_t, chans), BF16),) * (n_t - 1),
         in_specs=[whole(SMEM)] + [whole()] * (4 * n_z) + [whole(pltpu.HBM)] * 2,
-        out_specs=(whole(),) * 3,
+        out_specs=(whole(),) * (2 + n_t),
         scratch_shapes=[
             VMEM((slots, chans, min(ff, 1024)), BF16),
             VMEM((slots, chans, min(ff, 1024)), BF16),
@@ -479,13 +464,11 @@
     ff = gate_pre.shape[1]
     width = -(-ff // 256) * 128
 
-    def from_tensor(own):
-        return [own] + [
-            lax.ppermute(own, "tensor", [(a, a ^ s) for a in range(n_t)]) for s in range(1, n_t)
-        ]
+    def to_tensor(value, s):
+        return lax.ppermute(value, "tensor", [(p, p ^ s) for p in range(n_t)])
 
     both, rows = prep(xq, xs, xo, xc, gq, gs, go, gc, gate_pre, up_pre)
-    both = from_tensor(both)
+    both = [both] + [to_tensor(both, s) for s in range(1, n_t)]
     bit = n_z // 2
     rows = {0: rows, bit: to_chip(rows, bit, n_z), 1: to_chip(rows, 1, n_z)}
     grads, grads_t, *send = first_half(place, both, w_down, n_z, width)
@@ -503,12 +486,13 @@
     grad_down, token = down_grad(place, *gate_up, grads, ff - width, width, grad_down)
     hidden[bit] = add_all([(0, width, [(hidden[bit], None, 0)])], [token, hidden[1]])
     hidden = complete_z(hidden, n_z)
-    gate_grad, up_grad, sends = input_grad(
+    gate_grad, up_grad, kept, *sends = input_grad(
         place, (hidden, [to_core(part) for part in hidden]), gate_up, w_gate, w_up, n_t
     )
-    terms = lax.all_to_all(sends, "tensor", 0, 0, tiled=True)
+    terms = [kept] + [to_tensor(part, s) for s, part in enumerate(sends, 1)]
     grad_gate, grad_up = weight_grads(place, both, gate_grad, up_grad, n_z)
-    return sum_parts(terms), grad_gate, grad_up, grad_down
+    grad_input = add_all([(0, kept.shape[1], [(term, None, 0) for term in terms])], [])
+    return grad_input, grad_gate, grad_up, grad_down
 
 
 def solution(mesh):

time: 99.8 us -> 96.8 us (0.970)
  local copies, waits for them, and re-layouts: 3.24 us -> 0.9 us
    all_to_all x1 -> x0, starting transfers between devices: 3.58 us -> none  [on_device(): terms = lax.all_to_all(sends, 'tensor', 0, 0, tiled=True)]
    ppermute x3 -> x6, starting transfers between devices: 3.49 us -> 7.04 us  [to_tensor(): return lax.ppermute(value, 'tensor', [(p, p ^ s) for p in range(n_t)])]
    unnamed x10 -> x6, local copies, waits for them, and re-layouts: 3.24 us -> 0.9 us
    ppermute x3 -> x6, waiting for transfers between devices: 4.21 us -> 4.22 us  [to_tensor(): return lax.ppermute(value, 'tensor', [(p, p ^ s) for p in range(n_t)])]
  transfers between devices with their start and end apart: 24 -> 26, of which waited for: 10 -> 10; matrix products, arithmetic and copies ran while one was open for 0% -> 0% of each run, Pallas kernels for 32% -> 33%
where the time goes in v2:
time: 96.8 us; the launch traced here: 96.7 us
  Pallas kernels  48.6 us (50%)
  waiting for transfers between devices  25.8 us (27%)
  starting transfers between devices  20.5 us (21%)
    ppermute x8, waiting for transfers between devices, to_chip(): return lax.ppermute(value, 'z', [(a, a ^ bit) for a in range(n_z)])  20.2 us
    pallas_call x1, Pallas kernels, input_grad(): pl.pallas_call(functools.partial(input_kernel, n_z), out_shape=(shape((to...  13.8 us
    pallas_call x1, Pallas kernels, weight_grads(): pl.pallas_call(functools.partial(weight_kernel, n_z, n_t), out_shape=(sha...  11.7 us
    ppermute x8, starting transfers between devices, to_chip(): return lax.ppermute(value, 'z', [(a, a ^ bit) for a in range(n_z)])  11.1 us
    pallas_call x2, Pallas kernels, down_grad(): pl.pallas_call(functools.partial(down_kernel, base, ff, n_z), out_shape=(...  8.31 us
    ppermute x6, starting transfers between devices, to_tensor(): return lax.ppermute(value, 'tensor', [(p, p ^ s) for p in range(n_t)])  7.04 us
    pallas_call x1, Pallas kernels, second_half(): pl.pallas_call(functools.partial(second_half_kernel, offset, base), out_s...  5.68 us
    pallas_call x1, Pallas kernels, first_half(): pl.pallas_call(functools.partial(first_half_kernel, n_t, n_z, w_down.shap...  5.66 us
  transfers between devices with their start and end apart: 26, of which 10 were waited for; matrix products, arithmetic and copies ran while one was open for 0% of the time, Pallas kernels for 33%

profile of v2, /device:TPU:0, one launch (start us, length us, event | category | flops | bytes accessed | tf_op | source)
XLA Modules:
  0.0 96.7 jit_solution(10183684059790285124)
XLA Ops:
  0.6 2.0 %shard_map.156 = (bf16[2,24,1024]{2,1,0:T(8,128)(2,1)}, bf16[24,6656]{1,0:T(8,128)(2,1)}) custom-call(bf16[24,1024]{1,0:T(8,128)(2,1)} %xq.1, f32[1,8]{1,0:T(1,128)} %xs.1, s32[1,8]{1,0:T(1,128)} %xo.1, bf16[24,1024]{1,0:T(8,128)(2,1)} %xc.1, bf16[24,1024]{1,0:T(8,128)(2,1)} %gq.1, f32[1,8]{1,0:T(1,128)} %gs.1, s32[1,8]{1,0:T(1,128)} %go.1, ...), custom_call_target="tpu_custom_call" | custom-call | bytes 835584 | tf_op jit(solution)/shard_map/pallas_call | solution.py:58
  2.6 4.0 %collective-permute-start.4 = (bf16[24,6656]{1,0:T(8,128)(2,1)}, bf16[24,6656]{1,0:T(8,128)(2,1)S(1)}, u32[]{:S(2)}, u32[]{:S(2)}) collective-permute-start(bf16[24,6656]{1,0:T(8,128)(2,1)} %get-tuple-element.29.refs_0_.refs_8_), channel_id=1, source_target_pairs={{0,16},{8,24},{16,0},{24,8},{1,17},{9,25},{17,1},{25,9},{2,18},{10... | collective-permute-start | bytes 958472 | tf_op jit(solution)/shard_map/ppermute | solution.py:243
  6.7 1.6 %collective-permute-start.3 = (bf16[24,6656]{1,0:T(8,128)(2,1)}, bf16[24,6656]{1,0:T(8,128)(2,1)S(1)}, u32[]{:S(2)}, u32[]{:S(2)}) collective-permute-start(bf16[24,6656]{1,0:T(8,128)(2,1)} %get-tuple-element.29.refs_0_.refs_8_), channel_id=1, source_target_pairs={{0,8},{8,0},{16,24},{24,16},{1,9},{9,1},{17,25},{25,17},{2,10},{10... | collective-permute-start | bytes 958472 | tf_op jit(solution)/shard_map/ppermute | solution.py:243
  8.2 2.4 %collective-permute-start.2 = (bf16[2,24,1024]{2,1,0:T(8,128)(2,1)}, bf16[2,24,1024]{2,1,0:T(8,128)(2,1)S(1)}, u32[]{:S(2)}, u32[]{:S(2)}) collective-permute-start(bf16[2,24,1024]{2,1,0:T(8,128)(2,1)} %get-tuple-element.27.refs_0_), channel_id=1, source_target_pairs={{0,3},{1,2},{2,1},{3,0},{4,7},{5,6},{6,5},{7,4},{8,11},{9,10},{10,... | collective-permute-start | bytes 294920 | tf_op jit(solution)/shard_map/ppermute | solution.py:468
  11.8 2.5 %collective-permute-done.2.refs_3_ = bf16[2,24,1024]{2,1,0:T(8,128)(2,1)S(1)} collective-permute-done((bf16[2,24,1024]{2,1,0:T(8,128)(2,1)}, bf16[2,24,1024]{2,1,0:T(8,128)(2,1)S(1)}, u32[]{:S(2)}, u32[]{:S(2)}) %collective-permute-start.2) | collective-permute-done | bytes 98336 | tf_op jit(solution)/shard_map/ppermute | solution.py:468
  14.3 1.3 %collective-permute-done.1.refs_2_ = bf16[2,24,1024]{2,1,0:T(8,128)(2,1)S(1)} collective-permute-done((bf16[2,24,1024]{2,1,0:T(8,128)(2,1)}, bf16[2,24,1024]{2,1,0:T(8,128)(2,1)S(1)}, u32[]{:S(2)}, u32[]{:S(2)}) %collective-permute-start.1) | collective-permute-done | bytes 98336 | tf_op jit(solution)/shard_map/ppermute | solution.py:468
  16.0 0.9 copy-done.1
  16.9 5.7 %shard_map.157 = (bf16[96,1024]{1,0:T(8,128)(2,1)S(1)}, bf16[1024,96]{1,0:T(8,128)(2,1)S(1)}, bf16[24,3328]{1,0:T(8,128)(2,1)S(1)}, bf16[24,3328]{1,0:T(8,128)(2...) custom-call(s32[3]{0:T(128)S(1)} %pad_add_fusion.place, bf16[2,24,1024]{2,1,0:T(8,128)(2,1)S(1)} %copy-done.1, ...), custom_call_target="tpu_custom_call" | custom-call | flops 654311424 | bytes 6815744 | tf_op jit(solution)/shard_map/pallas_call | solution.py:145
  24.1 5.7 %shard_map.158.mine = f32[4,24,3328]{2,1,0:T(8,128)S(1)} custom-call(s32[3]{0:T(128)S(1)} %pad_add_fusion.place, bf16[1024,96]{1,0:T(8,128)(2,1)S(1)} %get-tuple-element.28.grads_t, bf16[6656,1024]{1,0:T(8,128)(2,1)} %w_hbm.1, bf16[24,6656]{1,0:T(8,128)(2,1)S(1)} %collective-permute-done.3.refs_0_.refs_1_.refs_9_, ...), custom_call_target="tpu_custom_call" | custom-call | flops 7851737088 | bytes 81788928 | tf_op jit(solution)/shard_map/pallas_call | solution.py:168
  31.2 1.6 %collective-permute-start.9 = (bf16[2,24,3328]{2,1,0:T(8,128)(2,1)S(1)}, bf16[2,24,3328]{2,1,0:T(8,128)(2,1)S(1)}, u32[]{:S(2)}, u32[]{:S(2)}) collective-permute-start(bf16[2,24,3328]{2,1,0:T(8,128)(2,1)S(1)} %get-tuple-element.35), channel_id=1, source_target_pairs={{0,8},{8,0},{16,24},{24,16},{1,9},{9,1},{17,25},{25,17},{2,10},{10... | collective-permute-start | bytes 958472 | tf_op jit(solution)/shard_map/ppermute | solution.py:243
  33.2 8.0 %collective-permute-done.9.refs_1_ = bf16[2,24,3328]{2,1,0:T(8,128)(2,1)S(1)} collective-permute-done((bf16[2,24,3328]{2,1,0:T(8,128)(2,1)S(1)}, bf16[2,24,3328]{2,1,0:T(8,128)(2,1)S(1)}, u32[]{:S(2)}, u32[]{:S(2)}) %collective-permute-start.9) | collective-permute-done | bytes 319520 | tf_op jit(solution)/shard_map/ppermute | solution.py:243
  41.2 1.3 %collective-permute-start.13 = (bf16[24,3328]{1,0:T(8,128)(2,1)S(1)}, bf16[24,3328]{1,0:T(8,128)(2,1)S(1)}, u32[]{:S(2)}, u32[]{:S(2)}) collective-permute-start(bf16[24,3328]{1,0:T(8,128)(2,1)S(1)} %shard_map.160), channel_id=1, source_target_pairs={{0,16},{8,24},{16,0},{24,8},{1,17},{9,25},{17,1},{25,9},{2,18},{10... | collective-permute-start | bytes 479240 | tf_op jit(solution)/shard_map/ppermute | solution.py:243
  42.5 4.2 %shard_map.161 = (bf16[6656,1024]{1,0:T(8,128)(2,1)}, f32[8,128]{1,0:T(8,128)S(1)}) custom-call(s32[3]{0:T(128)S(1)} %pad_add_fusion.place, bf16[24,6656]{1,0:T(8,128)(2,1)S(1)} %copy-done, bf16[24,6656]{1,0:T(8,128)(2,1)S(1)} %collective-permute-done.3.refs_0_.refs_1_.refs_9_, bf16[24,6656]{1,0:T(8,128)(2,1)S(1)} %collective-permute-done.4.refs_1_.refs_2_.refs_10_, ...), custom_call_target="tpu_custom_call" | custom-call | flops 654311424 | bytes 6815744 | tf_op jit(solution)/shard_map/pallas_call | solution.py:313
  46.7 4.6 %collective-permute-done.13.refs_2_ = bf16[24,3328]{1,0:T(8,128)(2,1)S(1)} collective-permute-done((bf16[24,3328]{1,0:T(8,128)(2,1)S(1)}, bf16[24,3328]{1,0:T(8,128)(2,1)S(1)}, u32[]{:S(2)}, u32[]{:S(2)}) %collective-permute-start.13) | collective-permute-done | bytes 159776 | tf_op jit(solution)/shard_map/ppermute | solution.py:243
  51.4 1.9 %collective-permute-start.16 = (bf16[24,3328]{1,0:T(8,128)(2,1)S(1)}, bf16[24,3328]{1,0:T(8,128)(2,1)S(1)}, u32[]{:S(2)}, u32[]{:S(2)}) collective-permute-start(bf16[24,3328]{1,0:T(8,128)(2,1)S(1)} %shard_map.162.refs_0_), channel_id=1, source_target_pairs={{0,8},{8,0},{16,24},{24,16},{1,9},{9,1},{17,25},{25,17},{2,10},{10... | collective-permute-start | bytes 479240 | tf_op jit(solution)/shard_map/ppermute | solution.py:243
  53.3 4.2 %shard_map.163 = (bf16[6656,1024]{1,0:T(8,128)(2,1)}, f32[8,128]{1,0:T(8,128)S(1)}) custom-call(s32[3]{0:T(128)S(1)} %pad_add_fusion.place, bf16[24,6656]{1,0:T(8,128)(2,1)S(1)} %copy-done, bf16[24,6656]{1,0:T(8,128)(2,1)S(1)} %collective-permute-done.3.refs_0_.refs_1_.refs_9_, ...), custom_call_target="tpu_custom_call", output_to_operand_aliasing={{0}: (10, {})} | custom-call | flops 654311424 | bytes 6815744 | tf_op jit(solution)/shard_map/pallas_call | solution.py:313
  57.5 2.4 %collective-permute-done.17.refs_0_ = bf16[24,3328]{1,0:T(8,128)(2,1)S(1)} collective-permute-done((bf16[24,3328]{1,0:T(8,128)(2,1)S(1)}, bf16[24,3328]{1,0:T(8,128)(2,1)S(1)}, u32[]{:S(2)}, u32[]{:S(2)}) %collective-permute-start.17) | collective-permute-done | bytes 159776 | tf_op jit(solution)/shard_map/ppermute | solution.py:243
  60.8 4.7 %collective-permute-done.18.refs_3_ = bf16[24,3328]{1,0:T(8,128)(2,1)S(1)} collective-permute-done((bf16[24,3328]{1,0:T(8,128)(2,1)S(1)}, bf16[24,3328]{1,0:T(8,128)(2,1)S(1)}, u32[]{:S(2)}, u32[]{:S(2)}) %collective-permute-start.18) | collective-permute-done | bytes 159776 | tf_op jit(solution)/shard_map/ppermute | solution.py:243
  65.6 1.4 %collective-permute-done.22.refs_7_ = bf16[24,3328]{1,0:T(8,128)(2,1)S(1)} collective-permute-done((bf16[24,3328]{1,0:T(8,128)(2,1)S(1)}, bf16[24,3328]{1,0:T(8,128)(2,1)S(1)}, u32[]{:S(2)}, u32[]{:S(2)}) %collective-permute-start.22) | collective-permute-done | bytes 159776 | tf_op jit(solution)/shard_map/ppermute | solution.py:247
  67.0 13.8 %shard_map.165 = (bf16[96,6656]{1,0:T(8,128)(2,1)S(1)}, bf16[96,6656]{1,0:T(8,128)(2,1)S(1)}, f32[24,1024]{1,0:T(8,128)S(1)}, bf16[24,1024]{1,0:T(8,128)(2,1)S(1...) custom-call(s32[3]{0:T(128)S(1)} %pad_add_fusion.place, bf16[24,3328]{1,0:T(8,128)(2,1)S(1)} %shard_map.162.refs_0_, ...), custom_call_target="tpu_custom_call" | custom-call | flops 2617245696 | bytes 34930688 | tf_op jit(solution)/shard_map/pallas_call | solution.py:402
  80.7 0.8 collective-permute-start.23
  81.6 1.2 %collective-permute-start.24 = (bf16[24,1024]{1,0:T(8,128)(2,1)S(1)}, bf16[24,1024]{1,0:T(8,128)(2,1)S(1)}, u32[]{:S(2)}, u32[]{:S(2)}) collective-permute-start(bf16[24,1024]{1,0:T(8,128)(2,1)S(1)} %get-tuple-element.43), channel_id=1, source_target_pairs={{0,2},{1,3},{2,0},{3,1},{4,6},{5,7},{6,4},{7,5},{8,10},{9,11},{10,... | collective-permute-start | bytes 147464 | tf_op jit(solution)/shard_map/ppermute | solution.py:468
  82.7 1.6 %collective-permute-start.25 = (bf16[24,1024]{1,0:T(8,128)(2,1)S(1)}, bf16[24,1024]{1,0:T(8,128)(2,1)S(1)}, u32[]{:S(2)}, u32[]{:S(2)}) collective-permute-start(bf16[24,1024]{1,0:T(8,128)(2,1)S(1)} %get-tuple-element.44), channel_id=1, source_target_pairs={{0,3},{1,2},{2,1},{3,0},{4,7},{5,6},{6,5},{7,4},{8,11},{9,10},{10,... | collective-permute-start | bytes 147464 | tf_op jit(solution)/shard_map/ppermute | solution.py:468
  84.3 11.7 %shard_map.167 = (bf16[1024,6656]{1,0:T(8,128)(2,1)}, bf16[1024,6656]{1,0:T(8,128)(2,1)}) custom-call(s32[3]{0:T(128)S(1)} %pad_add_fusion.place, bf16[2,24,1024]{2,1,0:T(8,128)(2,1)S(1)} %copy-done.2, bf16[2,24,1024]{2,1,0:T(8,128)(2,1)S(1)} %collective-permute-done.refs_1_, bf16[2,24,1024]{2,1,0:T(8,128)(2,1)S(1)} %collective-permute-done.1.refs_2_, ...), custom_call_target="tpu_custom_call" | custom-call | flops 2617245696 | bytes 29818880 | tf_op jit(solution)/shard_map/pallas_call | solution.py:446
  (47 shorter events, 6.5 us)
Async XLA Ops:
  2.6 20.6 %collective-permute-start.4 = (bf16[24,6656]{1,0:T(8,128)(2,1)}, bf16[24,6656]{1,0:T(8,128)(2,1)S(1)}, u32[]{:S(2)}, u32[]{:S(2)}) collective-permute-start(bf16[24,6656]{1,0:T(8,128)(2,1)} %get-tuple-element.29.refs_0_.refs_8_), channel_id=1, source_target_pairs={{0,16},{8,24},{16,0},{24,8},{1,17},{9,25},{17,1},{25,9},{2,18},{10... | collective-permute-start | bytes 958472 | tf_op jit(solution)/shard_map/ppermute | solution.py:243
  6.7 17.0 %collective-permute-start.3 = (bf16[24,6656]{1,0:T(8,128)(2,1)}, bf16[24,6656]{1,0:T(8,128)(2,1)S(1)}, u32[]{:S(2)}, u32[]{:S(2)}) collective-permute-start(bf16[24,6656]{1,0:T(8,128)(2,1)} %get-tuple-element.29.refs_0_.refs_8_), channel_id=1, source_target_pairs={{0,8},{8,0},{16,24},{24,16},{1,9},{9,1},{17,25},{25,17},{2,10},{10... | collective-permute-start | bytes 958472 | tf_op jit(solution)/shard_map/ppermute | solution.py:243
  8.2 6.1 %collective-permute-start.2 = (bf16[2,24,1024]{2,1,0:T(8,128)(2,1)}, bf16[2,24,1024]{2,1,0:T(8,128)(2,1)S(1)}, u32[]{:S(2)}, u32[]{:S(2)}) collective-permute-start(bf16[2,24,1024]{2,1,0:T(8,128)(2,1)} %get-tuple-element.27.refs_0_), channel_id=1, source_target_pairs={{0,3},{1,2},{2,1},{3,0},{4,7},{5,6},{6,5},{7,4},{8,11},{9,10},{10,... | collective-permute-start | bytes 294920 | tf_op jit(solution)/shard_map/ppermute | solution.py:468
  10.7 5.0 %collective-permute-start.1 = (bf16[2,24,1024]{2,1,0:T(8,128)(2,1)}, bf16[2,24,1024]{2,1,0:T(8,128)(2,1)S(1)}, u32[]{:S(2)}, u32[]{:S(2)}) collective-permute-start(bf16[2,24,1024]{2,1,0:T(8,128)(2,1)} %get-tuple-element.27.refs_0_), channel_id=1, source_target_pairs={{0,2},{1,3},{2,0},{3,1},{4,6},{5,7},{6,4},{7,5},{8,10},{9,11},{10,... | collective-permute-start | bytes 294920 | tf_op jit(solution)/shard_map/ppermute | solution.py:468
  11.2 4.8 %collective-permute-start = (bf16[2,24,1024]{2,1,0:T(8,128)(2,1)}, bf16[2,24,1024]{2,1,0:T(8,128)(2,1)S(1)}, u32[]{:S(2)}, u32[]{:S(2)}) collective-permute-start(bf16[2,24,1024]{2,1,0:T(8,128)(2,1)} %get-tuple-element.27.refs_0_), channel_id=1, source_target_pairs={{0,1},{1,0},{2,3},{3,2},{4,5},{5,4},{6,7},{7,6},{8,9},{9,8},{10,11... | collective-permute-start | bytes 294920 | tf_op jit(solution)/shard_map/ppermute | solution.py:468
  22.6 7.2 %collective-permute-start.5 = (bf16[24,3328]{1,0:T(8,128)(2,1)S(1)}, bf16[24,3328]{1,0:T(8,128)(2,1)S(1)}, u32[]{:S(2)}, u32[]{:S(2)}) collective-permute-start(bf16[24,3328]{1,0:T(8,128)(2,1)S(1)} %get-tuple-element.30), channel_id=1, source_target_pairs={{0,4},{4,0},{1,5},{5,1},{2,6},{6,2},{3,7},{7,3},{8,12},{12,8},{9,1... | collective-permute-start | bytes 479240 | tf_op jit(solution)/shard_map/ppermute | solution.py:247
  22.6 7.3 %collective-permute-start.6 = (bf16[24,3328]{1,0:T(8,128)(2,1)S(1)}, bf16[24,3328]{1,0:T(8,128)(2,1)S(1)}, u32[]{:S(2)}, u32[]{:S(2)}) collective-permute-start(bf16[24,3328]{1,0:T(8,128)(2,1)S(1)} %get-tuple-element.31), channel_id=1, source_target_pairs={{0,4},{4,0},{1,5},{5,1},{2,6},{6,2},{3,7},{7,3},{8,12},{12,8},{9,1... | collective-permute-start | bytes 479240 | tf_op jit(solution)/shard_map/ppermute | solution.py:247
  23.1 7.3 %collective-permute-start.7 = (bf16[24,3328]{1,0:T(8,128)(2,1)S(1)}, bf16[24,3328]{1,0:T(8,128)(2,1)S(1)}, u32[]{:S(2)}, u32[]{:S(2)}) collective-permute-start(bf16[24,3328]{1,0:T(8,128)(2,1)S(1)} %get-tuple-element.32), channel_id=1, source_target_pairs={{0,4},{4,0},{1,5},{5,1},{2,6},{6,2},{3,7},{7,3},{8,12},{12,8},{9,1... | collective-permute-start | bytes 479240 | tf_op jit(solution)/shard_map/ppermute | solution.py:247
  23.2 7.3 %collective-permute-start.8 = (bf16[24,3328]{1,0:T(8,128)(2,1)S(1)}, bf16[24,3328]{1,0:T(8,128)(2,1)S(1)}, u32[]{:S(2)}, u32[]{:S(2)}) collective-permute-start(bf16[24,3328]{1,0:T(8,128)(2,1)S(1)} %get-tuple-element.33), channel_id=1, source_target_pairs={{0,4},{4,0},{1,5},{5,1},{2,6},{6,2},{3,7},{7,3},{8,12},{12,8},{9,1... | collective-permute-start | bytes 479240 | tf_op jit(solution)/shard_map/ppermute | solution.py:247
  23.7 9.5 %collective-permute-start.14 = (bf16[24,6656]{1,0:T(8,128)(2,1)S(1)}, bf16[24,6656]{1,0:T(8,128)(2,1)S(1)}, u32[]{:S(2)}, u32[]{:S(2)}) collective-permute-start(bf16[24,6656]{1,0:T(8,128)(2,1)S(1)} %collective-permute-done.4.refs_1_.refs_2_.refs_10_), channel_id=1, source_target_pairs={{0,8},{8,0},{16,24},{24,16},{1,9},{9,1},{17,25},{25,17},{2,10},{10... | collective-permute-start | bytes 958472 | tf_op jit(solution)/shard_map/ppermute | solution.py:243
  29.8 3.4 %collective-permute-start.10 = (bf16[24,6656]{1,0:T(8,128)(2,1)S(1)}, bf16[24,6656]{1,0:T(8,128)(2,1)S(1)}, u32[]{:S(2)}, u32[]{:S(2)}) collective-permute-start(bf16[24,6656]{1,0:T(8,128)(2,1)S(1)} %copy-done), channel_id=1, source_target_pairs={{0,4},{4,0},{1,5},{5,1},{2,6},{6,2},{3,7},{7,3},{8,12},{12,8},{9,1... | collective-permute-start | bytes 958472 | tf_op jit(solution)/shard_map/ppermute | solution.py:247
  29.9 3.3 %collective-permute-start.12 = (bf16[24,6656]{1,0:T(8,128)(2,1)S(1)}, bf16[24,6656]{1,0:T(8,128)(2,1)S(1)}, u32[]{:S(2)}, u32[]{:S(2)}) collective-permute-start(bf16[24,6656]{1,0:T(8,128)(2,1)S(1)} %collective-permute-done.4.refs_1_.refs_2_.refs_10_), channel_id=1, source_target_pairs={{0,4},{4,0},{1,5},{5,1},{2,6},{6,2},{3,7},{7,3},{8,12},{12,8},{9,1... | collective-permute-start | bytes 958472 | tf_op jit(solution)/shard_map/ppermute | solution.py:247
  31.2 9.9 %collective-permute-start.9 = (bf16[2,24,3328]{2,1,0:T(8,128)(2,1)S(1)}, bf16[2,24,3328]{2,1,0:T(8,128)(2,1)S(1)}, u32[]{:S(2)}, u32[]{:S(2)}) collective-permute-start(bf16[2,24,3328]{2,1,0:T(8,128)(2,1)S(1)} %get-tuple-element.35), channel_id=1, source_target_pairs={{0,8},{8,0},{16,24},{24,16},{1,9},{9,1},{17,25},{25,17},{2,10},{10... | collective-permute-start | bytes 958472 | tf_op jit(solution)/shard_map/ppermute | solution.py:243
  33.2 9.3 %collective-permute-start.15 = (bf16[24,6656]{1,0:T(8,128)(2,1)S(1)}, bf16[24,6656]{1,0:T(8,128)(2,1)S(1)}, u32[]{:S(2)}, u32[]{:S(2)}) collective-permute-start(bf16[24,6656]{1,0:T(8,128)(2,1)S(1)} %collective-permute-done.14.refs_3_.refs_11_), channel_id=1, source_target_pairs={{0,4},{4,0},{1,5},{5,1},{2,6},{6,2},{3,7},{7,3},{8,12},{12,8},{9,1... | collective-permute-start | bytes 958472 | tf_op jit(solution)/shard_map/ppermute | solution.py:247
  41.2 10.1 %collective-permute-start.13 = (bf16[24,3328]{1,0:T(8,128)(2,1)S(1)}, bf16[24,3328]{1,0:T(8,128)(2,1)S(1)}, u32[]{:S(2)}, u32[]{:S(2)}) collective-permute-start(bf16[24,3328]{1,0:T(8,128)(2,1)S(1)} %shard_map.160), channel_id=1, source_target_pairs={{0,16},{8,24},{16,0},{24,8},{1,17},{9,25},{17,1},{25,9},{2,18},{10... | collective-permute-start | bytes 479240 | tf_op jit(solution)/shard_map/ppermute | solution.py:243
  51.3 8.6 %collective-permute-start.17 = (bf16[24,3328]{1,0:T(8,128)(2,1)S(1)}, bf16[24,3328]{1,0:T(8,128)(2,1)S(1)}, u32[]{:S(2)}, u32[]{:S(2)}) collective-permute-start(bf16[24,3328]{1,0:T(8,128)(2,1)S(1)} %shard_map.162.refs_0_), channel_id=1, source_target_pairs={{0,16},{8,24},{16,0},{24,8},{1,17},{9,25},{17,1},{25,9},{2,18},{10... | collective-permute-start | bytes 479240 | tf_op jit(solution)/shard_map/ppermute | solution.py:243
  51.4 8.7 %collective-permute-start.16 = (bf16[24,3328]{1,0:T(8,128)(2,1)S(1)}, bf16[24,3328]{1,0:T(8,128)(2,1)S(1)}, u32[]{:S(2)}, u32[]{:S(2)}) collective-permute-start(bf16[24,3328]{1,0:T(8,128)(2,1)S(1)} %shard_map.162.refs_0_), channel_id=1, source_target_pairs={{0,8},{8,0},{16,24},{24,16},{1,9},{9,1},{17,25},{25,17},{2,10},{10... | collective-permute-start | bytes 479240 | tf_op jit(solution)/shard_map/ppermute | solution.py:243
  60.1 5.5 %collective-permute-start.18 = (bf16[24,3328]{1,0:T(8,128)(2,1)S(1)}, bf16[24,3328]{1,0:T(8,128)(2,1)S(1)}, u32[]{:S(2)}, u32[]{:S(2)}) collective-permute-start(bf16[24,3328]{1,0:T(8,128)(2,1)S(1)} %shard_map.164.refs_2_), channel_id=1, source_target_pairs={{0,8},{8,0},{16,24},{24,16},{1,9},{9,1},{17,25},{25,17},{2,10},{10... | collective-permute-start | bytes 479240 | tf_op jit(solution)/shard_map/ppermute | solution.py:243
  60.2 5.4 %collective-permute-start.19 = (bf16[24,3328]{1,0:T(8,128)(2,1)S(1)}, bf16[24,3328]{1,0:T(8,128)(2,1)S(1)}, u32[]{:S(2)}, u32[]{:S(2)}) collective-permute-start(bf16[24,3328]{1,0:T(8,128)(2,1)S(1)} %shard_map.162.refs_0_), channel_id=1, source_target_pairs={{0,4},{4,0},{1,5},{5,1},{2,6},{6,2},{3,7},{7,3},{8,12},{12,8},{9,1... | collective-permute-start | bytes 479240 | tf_op jit(solution)/shard_map/ppermute | solution.py:247
  60.3 5.3 %collective-permute-start.21 = (bf16[24,3328]{1,0:T(8,128)(2,1)S(1)}, bf16[24,3328]{1,0:T(8,128)(2,1)S(1)}, u32[]{:S(2)}, u32[]{:S(2)}) collective-permute-start(bf16[24,3328]{1,0:T(8,128)(2,1)S(1)} %shard_map.164.refs_2_), channel_id=1, source_target_pairs={{0,4},{4,0},{1,5},{5,1},{2,6},{6,2},{3,7},{7,3},{8,12},{12,8},{9,1... | collective-permute-start | bytes 479240 | tf_op jit(solution)/shard_map/ppermute | solution.py:247
  60.8 4.8 %collective-permute-start.20 = (bf16[24,3328]{1,0:T(8,128)(2,1)S(1)}, bf16[24,3328]{1,0:T(8,128)(2,1)S(1)}, u32[]{:S(2)}, u32[]{:S(2)}) collective-permute-start(bf16[24,3328]{1,0:T(8,128)(2,1)S(1)} %collective-permute-done.16.refs_2_.refs_1_), channel_id=1, source_target_pairs={{0,4},{4,0},{1,5},{5,1},{2,6},{6,2},{3,7},{7,3},{8,12},{12,8},{9,1... | collective-permute-start | bytes 479240 | tf_op jit(solution)/shard_map/ppermute | solution.py:247
  80.7 15.3 %collective-permute-start.23 = (bf16[24,1024]{1,0:T(8,128)(2,1)S(1)}, bf16[24,1024]{1,0:T(8,128)(2,1)S(1)}, u32[]{:S(2)}, u32[]{:S(2)}) collective-permute-start(bf16[24,1024]{1,0:T(8,128)(2,1)S(1)} %get-tuple-element.42), channel_id=1, source_target_pairs={{0,1},{1,0},{2,3},{3,2},{4,5},{5,4},{6,7},{7,6},{8,9},{9,8},{10,11... | collective-permute-start | bytes 147464 | tf_op jit(solution)/shard_map/ppermute | solution.py:468
  81.6 14.4 %collective-permute-start.24 = (bf16[24,1024]{1,0:T(8,128)(2,1)S(1)}, bf16[24,1024]{1,0:T(8,128)(2,1)S(1)}, u32[]{:S(2)}, u32[]{:S(2)}) collective-permute-start(bf16[24,1024]{1,0:T(8,128)(2,1)S(1)} %get-tuple-element.43), channel_id=1, source_target_pairs={{0,2},{1,3},{2,0},{3,1},{4,6},{5,7},{6,4},{7,5},{8,10},{9,11},{10,... | collective-permute-start | bytes 147464 | tf_op jit(solution)/shard_map/ppermute | solution.py:468
  82.7 13.3 %collective-permute-start.25 = (bf16[24,1024]{1,0:T(8,128)(2,1)S(1)}, bf16[24,1024]{1,0:T(8,128)(2,1)S(1)}, u32[]{:S(2)}, u32[]{:S(2)}) collective-permute-start(bf16[24,1024]{1,0:T(8,128)(2,1)S(1)} %get-tuple-element.44), channel_id=1, source_target_pairs={{0,3},{1,2},{2,1},{3,0},{4,7},{5,6},{6,5},{7,4},{8,11},{9,10},{10,... | collective-permute-start | bytes 147464 | tf_op jit(solution)/shard_map/ppermute | solution.py:468
  (5 other events, 35.0 us)

commit v3 on v2

--- a/solution.py
+++ b/solution.py
@@ -158,7 +158,7 @@
             pltpu.SemaphoreType.DMA((n_copies,)),
         ],
         compiler_params=params(44),
-        cost_estimate=cost(2 * tokens * chans * width, 2 * chans * width),
+        cost_estimate=cost(12 * tokens * chans * width, 12 * chans * width),
     )(place, *parts, w_down, *done)
 
 
@@ -418,10 +418,26 @@
     )(place, *hidden[0], *hidden[1], *gate_up[0], *gate_up[1], w_gate, w_up)
 
 
-def weight_kernel(n_z, n_t, place, *refs):
-    gate_grad, up_grad, gate_hbm, up_hbm, out, held, inputs_t, sems = refs[n_t:]
+def turn_kernel(n_z, n_t, place, *refs):
+    inputs_t, held = refs[-2:]
     hold(refs[:n_t], 1, place[2], held)
     inputs_t[...] = blocks_of(held, place[1], n_z).T.astype(BF16)
+
+
+def turn_inputs(place, parts, n_z):
+    n_t, (_, rows, chans) = len(parts), parts[0].shape
+    return pl.pallas_call(
+        functools.partial(turn_kernel, n_z, n_t),
+        out_shape=shape((chans, n_t * rows), BF16),
+        in_specs=[whole(SMEM)] + [whole()] * n_t,
+        out_specs=whole(),
+        scratch_shapes=[VMEM((n_t * rows, chans), F32)],
+        compiler_params=params(4),
+        cost_estimate=cost(0, n_t * rows * chans * 4),
+    )(place, *parts)
+
+
+def weight_kernel(inputs_t, gate_grad, up_grad, gate_hbm, up_hbm, out, sems):
     copies = []
     ff, slots = gate_grad.shape[1], out.shape[0]
     for grad, hbm in ((gate_grad, gate_hbm), (up_grad, up_hbm)):
@@ -439,24 +455,19 @@
         copy.wait()
 
 
-def weight_grads(place, parts, gate_grad, up_grad, n_z):
-    n_t, chans, tokens = len(parts), parts[0].shape[2], gate_grad.shape[0]
+def weight_grads(inputs_t, gate_grad, up_grad):
+    chans, tokens = inputs_t.shape
     ff = gate_grad.shape[1]
     slots = min(8, 2 * len(pieces(ff, 512)))
     return pl.pallas_call(
-        functools.partial(weight_kernel, n_z, n_t),
+        weight_kernel,
         out_shape=(shape((chans, ff), BF16),) * 2,
-        in_specs=[whole(SMEM)] + [whole()] * (n_t + 2),
+        in_specs=[whole()] * 3,
         out_specs=(whole(pltpu.HBM),) * 2,
-        scratch_shapes=[
-            VMEM((slots, chans, 512), BF16),
-            VMEM((tokens, chans), F32),
-            VMEM((chans, tokens), BF16),
-            pltpu.SemaphoreType.DMA((slots,)),
-        ],
+        scratch_shapes=[VMEM((slots, chans, 512), BF16), pltpu.SemaphoreType.DMA((slots,))],
         compiler_params=params(16),
         cost_estimate=cost(4 * tokens * chans * ff, 4 * chans * ff + 4 * tokens * ff),
-    )(place, *parts, gate_grad, up_grad)
+    )(inputs_t, gate_grad, up_grad)
 
 
 def on_device(n_z, n_t, xq, xs, xo, xc, gq, gs, go, gc, gate_pre, up_pre, w_gate, w_up, w_down):
@@ -481,7 +492,8 @@
     gate_up = (rows, [to_core(part) for part in rows])
     grad_down, token = down_grad(place, *gate_up, grads, 0, ff - width)
     early = [part for m, part in enumerate(gate_up[1]) if m != bit | 1]
-    hidden = {0: reduce_z(spans, n_z, (early, [token]))}
+    inputs_t = turn_inputs(place, both, n_z)
+    hidden = {0: reduce_z(spans, n_z, ([inputs_t, *early], [token]))}
     hidden |= {bit: to_chip(hidden[0], bit, n_z), 1: to_chip(hidden[0], 1, n_z)}
     grad_down, token = down_grad(place, *gate_up, grads, ff - width, width, grad_down)
     hidden[bit] = add_all([(0, width, [(hidden[bit], None, 0)])], [token, hidden[1]])
@@ -490,7 +502,7 @@
         place, (hidden, [to_core(part) for part in hidden]), gate_up, w_gate, w_up, n_t
     )
     terms = [kept] + [to_tensor(part, s) for s, part in enumerate(sends, 1)]
-    grad_gate, grad_up = weight_grads(place, both, gate_grad, up_grad, n_z)
+    grad_gate, grad_up = weight_grads(inputs_t, gate_grad, up_grad)
     grad_input = add_all([(0, kept.shape[1], [(term, None, 0) for term in terms])], [])
     return grad_input, grad_gate, grad_up, grad_down
 

time: 96.8 us -> 98.4 us (1.017)
  starting transfers between devices: 20.5 us -> 21.8 us
    ppermute x8, waiting for transfers between devices: 20.2 us -> 24.5 us  [to_chip(): return lax.ppermute(value, 'z', [(a, a ^ bit) for a in range(n_z)])]
    ppermute x6, waiting for transfers between devices: 4.22 us -> 0.16 us  [to_tensor(): return lax.ppermute(value, 'tensor', [(p, p ^ s) for p in range(n_t)])]
    ppermute x6, starting transfers between devices: 7.04 us -> 8.04 us  [to_tensor(): return lax.ppermute(value, 'tensor', [(p, p ^ s) for p in range(n_t)])]
    pallas_call x1 -> x2, Pallas kernels: 11.7 us -> 11.7 us  [the longest x1 11 us: weight_grads(): pl.pallas_call(weight_kernel, out_shape=(shape((chans, ff), BF16),) * 2,...]
where the time goes in v3:
time: 98.4 us; the launch traced here: 98.3 us
  Pallas kernels  48.6 us (49%)
  waiting for transfers between devices  26.1 us (27%)
  starting transfers between devices  21.8 us (22%)
    ppermute x8, waiting for transfers between devices, to_chip(): return lax.ppermute(value, 'z', [(a, a ^ bit) for a in range(n_z)])  24.5 us
    pallas_call x1, Pallas kernels, input_grad(): pl.pallas_call(functools.partial(input_kernel, n_z), out_shape=(shape((to...  13.8 us
    ppermute x8, starting transfers between devices, to_chip(): return lax.ppermute(value, 'z', [(a, a ^ bit) for a in range(n_z)])  11.9 us
    pallas_call x1, Pallas kernels, weight_grads(): pl.pallas_call(weight_kernel, out_shape=(shape((chans, ff), BF16),) * 2,...  11 us
    pallas_call x2, Pallas kernels, down_grad(): pl.pallas_call(functools.partial(down_kernel, base, ff, n_z), out_shape=(...  8.31 us
    ppermute x6, starting transfers between devices, to_tensor(): return lax.ppermute(value, 'tensor', [(p, p ^ s) for p in range(n_t)])  8.04 us
    pallas_call x1, Pallas kernels, second_half(): pl.pallas_call(functools.partial(second_half_kernel, offset, base), out_s...  5.68 us
    pallas_call x1, Pallas kernels, first_half(): pl.pallas_call(functools.partial(first_half_kernel, n_t, n_z, w_down.shap...  5.66 us
  transfers between devices with their start and end apart: 26, of which 10 were waited for; matrix products, arithmetic and copies ran while one was open for 0% of the time, Pallas kernels for 33%

profile of v3, /device:TPU:0, one launch (start us, length us, event | category | flops | bytes accessed | tf_op | source)
XLA Modules:
  0.0 98.3 jit_solution(5418142270641824320)
XLA Ops:
  0.6 2.0 %shard_map.156 = (bf16[2,24,1024]{2,1,0:T(8,128)(2,1)}, bf16[24,6656]{1,0:T(8,128)(2,1)}) custom-call(bf16[24,1024]{1,0:T(8,128)(2,1)} %xq.1, f32[1,8]{1,0:T(1,128)} %xs.1, s32[1,8]{1,0:T(1,128)} %xo.1, bf16[24,1024]{1,0:T(8,128)(2,1)} %xc.1, bf16[24,1024]{1,0:T(8,128)(2,1)} %gq.1, f32[1,8]{1,0:T(1,128)} %gs.1, s32[1,8]{1,0:T(1,128)} %go.1, ...), custom_call_target="tpu_custom_call" | custom-call | bytes 835584 | tf_op jit(solution)/shard_map/pallas_call | solution.py:58
  2.6 3.9 %collective-permute-start.2 = (bf16[2,24,1024]{2,1,0:T(8,128)(2,1)}, bf16[2,24,1024]{2,1,0:T(8,128)(2,1)S(1)}, u32[]{:S(2)}, u32[]{:S(2)}) collective-permute-start(bf16[2,24,1024]{2,1,0:T(8,128)(2,1)} %get-tuple-element.27.refs_0_), channel_id=1, source_target_pairs={{0,3},{1,2},{2,1},{3,0},{4,7},{5,6},{6,5},{7,4},{8,11},{9,10},{10,... | collective-permute-start | bytes 294920 | tf_op jit(solution)/shard_map/ppermute | solution.py:479
  7.1 3.0 %collective-permute-start.4 = (bf16[24,6656]{1,0:T(8,128)(2,1)}, bf16[24,6656]{1,0:T(8,128)(2,1)S(1)}, u32[]{:S(2)}, u32[]{:S(2)}) collective-permute-start(bf16[24,6656]{1,0:T(8,128)(2,1)} %get-tuple-element.29.refs_0_.refs_8_), channel_id=1, source_target_pairs={{0,16},{8,24},{16,0},{24,8},{1,17},{9,25},{17,1},{25,9},{2,18},{10... | collective-permute-start | bytes 958472 | tf_op jit(solution)/shard_map/ppermute | solution.py:243
  10.1 1.6 %collective-permute-start.3 = (bf16[24,6656]{1,0:T(8,128)(2,1)}, bf16[24,6656]{1,0:T(8,128)(2,1)S(1)}, u32[]{:S(2)}, u32[]{:S(2)}) collective-permute-start(bf16[24,6656]{1,0:T(8,128)(2,1)} %get-tuple-element.29.refs_0_.refs_8_), channel_id=1, source_target_pairs={{0,8},{8,0},{16,24},{24,16},{1,9},{9,1},{17,25},{25,17},{2,10},{10... | collective-permute-start | bytes 958472 | tf_op jit(solution)/shard_map/ppermute | solution.py:243
  12.0 0.9 copy-done.1
  12.8 5.7 %shard_map.157 = (bf16[96,1024]{1,0:T(8,128)(2,1)S(1)}, bf16[1024,96]{1,0:T(8,128)(2,1)S(1)}, bf16[24,3328]{1,0:T(8,128)(2,1)S(1)}, bf16[24,3328]{1,0:T(8,128)(2...) custom-call(s32[3]{0:T(128)S(1)} %pad_add_fusion.place, bf16[2,24,1024]{2,1,0:T(8,128)(2,1)S(1)} %copy-done.1, ...), custom_call_target="tpu_custom_call" | custom-call | flops 3925868544 | bytes 40894464 | tf_op jit(solution)/shard_map/pallas_call | solution.py:145
  19.2 4.8 %collective-permute-done.4.refs_1_.refs_2_.refs_10_ = bf16[24,6656]{1,0:T(8,128)(2,1)S(1)} collective-permute-done((bf16[24,6656]{1,0:T(8,128)(2,1)}, bf16[24,6656]{1,0:T(8,128)(2,1)S(1)}, u32[]{:S(2)}, u32[]{:S(2)}) %collective-permute-start.4) | collective-permute-done | bytes 319520 | tf_op jit(solution)/shard_map/ppermute | solution.py:243
  24.2 1.5 %collective-permute-start.14 = (bf16[24,6656]{1,0:T(8,128)(2,1)S(1)}, bf16[24,6656]{1,0:T(8,128)(2,1)S(1)}, u32[]{:S(2)}, u32[]{:S(2)}) collective-permute-start(bf16[24,6656]{1,0:T(8,128)(2,1)S(1)} %collective-permute-done.4.refs_1_.refs_2_.refs_10_), channel_id=1, source_target_pairs={{0,8},{8,0},{16,24},{24,16},{1,9},{9,1},{17,25},{25,17},{2,10},{10... | collective-permute-start | bytes 958472 | tf_op jit(solution)/shard_map/ppermute | solution.py:243
  25.7 5.7 %shard_map.158.mine = f32[4,24,3328]{2,1,0:T(8,128)S(1)} custom-call(s32[3]{0:T(128)S(1)} %pad_add_fusion.place, bf16[1024,96]{1,0:T(8,128)(2,1)S(1)} %get-tuple-element.28.grads_t, bf16[6656,1024]{1,0:T(8,128)(2,1)} %w_hbm.1, bf16[24,6656]{1,0:T(8,128)(2,1)S(1)} %collective-permute-done.3.refs_0_.refs_1_.refs_9_, ...), custom_call_target="tpu_custom_call" | custom-call | flops 7851737088 | bytes 81788928 | tf_op jit(solution)/shard_map/pallas_call | solution.py:168
  32.1 0.7 shard_map.159
  34.7 8.0 %collective-permute-done.9.refs_1_ = bf16[2,24,3328]{2,1,0:T(8,128)(2,1)S(1)} collective-permute-done((bf16[2,24,3328]{2,1,0:T(8,128)(2,1)S(1)}, bf16[2,24,3328]{2,1,0:T(8,128)(2,1)S(1)}, u32[]{:S(2)}, u32[]{:S(2)}) %collective-permute-start.9) | collective-permute-done | bytes 319520 | tf_op jit(solution)/shard_map/ppermute | solution.py:243
  42.8 2.4 %collective-permute-start.13 = (bf16[24,3328]{1,0:T(8,128)(2,1)S(1)}, bf16[24,3328]{1,0:T(8,128)(2,1)S(1)}, u32[]{:S(2)}, u32[]{:S(2)}) collective-permute-start(bf16[24,3328]{1,0:T(8,128)(2,1)S(1)} %shard_map.161), channel_id=1, source_target_pairs={{0,16},{8,24},{16,0},{24,8},{1,17},{9,25},{17,1},{25,9},{2,18},{10... | collective-permute-start | bytes 479240 | tf_op jit(solution)/shard_map/ppermute | solution.py:243
  45.2 4.2 %shard_map.162 = (bf16[6656,1024]{1,0:T(8,128)(2,1)}, f32[8,128]{1,0:T(8,128)S(1)}) custom-call(s32[3]{0:T(128)S(1)} %pad_add_fusion.place, bf16[24,6656]{1,0:T(8,128)(2,1)S(1)} %copy-done, bf16[24,6656]{1,0:T(8,128)(2,1)S(1)} %collective-permute-done.3.refs_0_.refs_1_.refs_9_, bf16[24,6656]{1,0:T(8,128)(2,1)S(1)} %collective-permute-done.4.refs_1_.refs_2_.refs_10_, ...), custom_call_target="tpu_custom_call" | custom-call | flops 654311424 | bytes 6815744 | tf_op jit(solution)/shard_map/pallas_call | solution.py:313
  49.3 3.5 %collective-permute-done.13.refs_2_ = bf16[24,3328]{1,0:T(8,128)(2,1)S(1)} collective-permute-done((bf16[24,3328]{1,0:T(8,128)(2,1)S(1)}, bf16[24,3328]{1,0:T(8,128)(2,1)S(1)}, u32[]{:S(2)}, u32[]{:S(2)}) %collective-permute-start.13) | collective-permute-done | bytes 159776 | tf_op jit(solution)/shard_map/ppermute | solution.py:243
  52.9 2.4 %collective-permute-start.16 = (bf16[24,3328]{1,0:T(8,128)(2,1)S(1)}, bf16[24,3328]{1,0:T(8,128)(2,1)S(1)}, u32[]{:S(2)}, u32[]{:S(2)}) collective-permute-start(bf16[24,3328]{1,0:T(8,128)(2,1)S(1)} %shard_map.163.refs_0_), channel_id=1, source_target_pairs={{0,8},{8,0},{16,24},{24,16},{1,9},{9,1},{17,25},{25,17},{2,10},{10... | collective-permute-start | bytes 479240 | tf_op jit(solution)/shard_map/ppermute | solution.py:243
  55.4 4.2 %shard_map.164 = (bf16[6656,1024]{1,0:T(8,128)(2,1)}, f32[8,128]{1,0:T(8,128)S(1)}) custom-call(s32[3]{0:T(128)S(1)} %pad_add_fusion.place, bf16[24,6656]{1,0:T(8,128)(2,1)S(1)} %copy-done, bf16[24,6656]{1,0:T(8,128)(2,1)S(1)} %collective-permute-done.3.refs_0_.refs_1_.refs_9_, ...), custom_call_target="tpu_custom_call", output_to_operand_aliasing={{0}: (10, {})} | custom-call | flops 654311424 | bytes 6815744 | tf_op jit(solution)/shard_map/pallas_call | solution.py:313
  59.6 2.1 %collective-permute-done.17.refs_0_ = bf16[24,3328]{1,0:T(8,128)(2,1)S(1)} collective-permute-done((bf16[24,3328]{1,0:T(8,128)(2,1)S(1)}, bf16[24,3328]{1,0:T(8,128)(2,1)S(1)}, u32[]{:S(2)}, u32[]{:S(2)}) %collective-permute-start.17) | collective-permute-done | bytes 159776 | tf_op jit(solution)/shard_map/ppermute | solution.py:243
  61.6 0.9 collective-permute-done.16.refs_2_.refs_1_
  63.3 4.5 %collective-permute-done.18.refs_3_ = bf16[24,3328]{1,0:T(8,128)(2,1)S(1)} collective-permute-done((bf16[24,3328]{1,0:T(8,128)(2,1)S(1)}, bf16[24,3328]{1,0:T(8,128)(2,1)S(1)}, u32[]{:S(2)}, u32[]{:S(2)}) %collective-permute-start.18) | collective-permute-done | bytes 159776 | tf_op jit(solution)/shard_map/ppermute | solution.py:243
  67.8 1.4 %collective-permute-done.22.refs_7_ = bf16[24,3328]{1,0:T(8,128)(2,1)S(1)} collective-permute-done((bf16[24,3328]{1,0:T(8,128)(2,1)S(1)}, bf16[24,3328]{1,0:T(8,128)(2,1)S(1)}, u32[]{:S(2)}, u32[]{:S(2)}) %collective-permute-start.22) | collective-permute-done | bytes 159776 | tf_op jit(solution)/shard_map/ppermute | solution.py:247
  69.2 13.8 %shard_map.166 = (bf16[96,6656]{1,0:T(8,128)(2,1)S(1)}, bf16[96,6656]{1,0:T(8,128)(2,1)S(1)}, f32[24,1024]{1,0:T(8,128)S(1)}, bf16[24,1024]{1,0:T(8,128)(2,1)S(1...) custom-call(s32[3]{0:T(128)S(1)} %pad_add_fusion.place, bf16[24,3328]{1,0:T(8,128)(2,1)S(1)} %shard_map.163.refs_0_, ...), custom_call_target="tpu_custom_call" | custom-call | flops 2617245696 | bytes 34930688 | tf_op jit(solution)/shard_map/pallas_call | solution.py:402
  83.0 1.6 %collective-permute-start.23 = (bf16[24,1024]{1,0:T(8,128)(2,1)S(1)}, bf16[24,1024]{1,0:T(8,128)(2,1)S(1)}, u32[]{:S(2)}, u32[]{:S(2)}) collective-permute-start(bf16[24,1024]{1,0:T(8,128)(2,1)S(1)} %get-tuple-element.42), channel_id=1, source_target_pairs={{0,1},{1,0},{2,3},{3,2},{4,5},{5,4},{6,7},{7,6},{8,9},{9,8},{10,11... | collective-permute-start | bytes 147464 | tf_op jit(solution)/shard_map/ppermute | solution.py:479
  84.5 1.5 %collective-permute-start.24 = (bf16[24,1024]{1,0:T(8,128)(2,1)S(1)}, bf16[24,1024]{1,0:T(8,128)(2,1)S(1)}, u32[]{:S(2)}, u32[]{:S(2)}) collective-permute-start(bf16[24,1024]{1,0:T(8,128)(2,1)S(1)} %get-tuple-element.43), channel_id=1, source_target_pairs={{0,2},{1,3},{2,0},{3,1},{4,6},{5,7},{6,4},{7,5},{8,10},{9,11},{10,... | collective-permute-start | bytes 147464 | tf_op jit(solution)/shard_map/ppermute | solution.py:479
  86.5 11.0 %shard_map.168 = (bf16[1024,6656]{1,0:T(8,128)(2,1)}, bf16[1024,6656]{1,0:T(8,128)(2,1)}) custom-call(bf16[1024,96]{1,0:T(8,128)(2,1)S(1)} %shard_map.160.refs_2_.inputs_t, bf16[96,6656]{1,0:T(8,128)(2,1)S(1)} %get-tuple-element.45.gate_grad, bf16[96,6656]{1,0:T(8,128)(2,1)S(1)} %get-tuple-element.46.up_grad), custom_call_target="tpu_custom_call" | custom-call | flops 2617245696 | bytes 29818880 | tf_op jit(solution)/shard_map/pallas_call | solution.py:462
  (48 shorter events, 6.3 us)
Async XLA Ops:
  2.6 9.2 %collective-permute-start.2 = (bf16[2,24,1024]{2,1,0:T(8,128)(2,1)}, bf16[2,24,1024]{2,1,0:T(8,128)(2,1)S(1)}, u32[]{:S(2)}, u32[]{:S(2)}) collective-permute-start(bf16[2,24,1024]{2,1,0:T(8,128)(2,1)} %get-tuple-element.27.refs_0_), channel_id=1, source_target_pairs={{0,3},{1,2},{2,1},{3,0},{4,7},{5,6},{6,5},{7,4},{8,11},{9,10},{10,... | collective-permute-start | bytes 294920 | tf_op jit(solution)/shard_map/ppermute | solution.py:479
  6.5 5.3 %collective-permute-start.1 = (bf16[2,24,1024]{2,1,0:T(8,128)(2,1)}, bf16[2,24,1024]{2,1,0:T(8,128)(2,1)S(1)}, u32[]{:S(2)}, u32[]{:S(2)}) collective-permute-start(bf16[2,24,1024]{2,1,0:T(8,128)(2,1)} %get-tuple-element.27.refs_0_), channel_id=1, source_target_pairs={{0,2},{1,3},{2,0},{3,1},{4,6},{5,7},{6,4},{7,5},{8,10},{9,11},{10,... | collective-permute-start | bytes 294920 | tf_op jit(solution)/shard_map/ppermute | solution.py:479
  7.0 4.9 %collective-permute-start = (bf16[2,24,1024]{2,1,0:T(8,128)(2,1)}, bf16[2,24,1024]{2,1,0:T(8,128)(2,1)S(1)}, u32[]{:S(2)}, u32[]{:S(2)}) collective-permute-start(bf16[2,24,1024]{2,1,0:T(8,128)(2,1)} %get-tuple-element.27.refs_0_), channel_id=1, source_target_pairs={{0,1},{1,0},{2,3},{3,2},{4,5},{5,4},{6,7},{7,6},{8,9},{9,8},{10,11... | collective-permute-start | bytes 294920 | tf_op jit(solution)/shard_map/ppermute | solution.py:479
  7.1 16.9 %collective-permute-start.4 = (bf16[24,6656]{1,0:T(8,128)(2,1)}, bf16[24,6656]{1,0:T(8,128)(2,1)S(1)}, u32[]{:S(2)}, u32[]{:S(2)}) collective-permute-start(bf16[24,6656]{1,0:T(8,128)(2,1)} %get-tuple-element.29.refs_0_.refs_8_), channel_id=1, source_target_pairs={{0,16},{8,24},{16,0},{24,8},{1,17},{9,25},{17,1},{25,9},{2,18},{10... | collective-permute-start | bytes 958472 | tf_op jit(solution)/shard_map/ppermute | solution.py:243
  10.1 14.0 %collective-permute-start.3 = (bf16[24,6656]{1,0:T(8,128)(2,1)}, bf16[24,6656]{1,0:T(8,128)(2,1)S(1)}, u32[]{:S(2)}, u32[]{:S(2)}) collective-permute-start(bf16[24,6656]{1,0:T(8,128)(2,1)} %get-tuple-element.29.refs_0_.refs_8_), channel_id=1, source_target_pairs={{0,8},{8,0},{16,24},{24,16},{1,9},{9,1},{17,25},{25,17},{2,10},{10... | collective-permute-start | bytes 958472 | tf_op jit(solution)/shard_map/ppermute | solution.py:243
  18.5 12.9 %collective-permute-start.5 = (bf16[24,3328]{1,0:T(8,128)(2,1)S(1)}, bf16[24,3328]{1,0:T(8,128)(2,1)S(1)}, u32[]{:S(2)}, u32[]{:S(2)}) collective-permute-start(bf16[24,3328]{1,0:T(8,128)(2,1)S(1)} %get-tuple-element.30), channel_id=1, source_target_pairs={{0,4},{4,0},{1,5},{5,1},{2,6},{6,2},{3,7},{7,3},{8,12},{12,8},{9,1... | collective-permute-start | bytes 479240 | tf_op jit(solution)/shard_map/ppermute | solution.py:247
  18.6 12.9 %collective-permute-start.6 = (bf16[24,3328]{1,0:T(8,128)(2,1)S(1)}, bf16[24,3328]{1,0:T(8,128)(2,1)S(1)}, u32[]{:S(2)}, u32[]{:S(2)}) collective-permute-start(bf16[24,3328]{1,0:T(8,128)(2,1)S(1)} %get-tuple-element.31), channel_id=1, source_target_pairs={{0,4},{4,0},{1,5},{5,1},{2,6},{6,2},{3,7},{7,3},{8,12},{12,8},{9,1... | collective-permute-start | bytes 479240 | tf_op jit(solution)/shard_map/ppermute | solution.py:247
  19.1 12.9 %collective-permute-start.7 = (bf16[24,3328]{1,0:T(8,128)(2,1)S(1)}, bf16[24,3328]{1,0:T(8,128)(2,1)S(1)}, u32[]{:S(2)}, u32[]{:S(2)}) collective-permute-start(bf16[24,3328]{1,0:T(8,128)(2,1)S(1)} %get-tuple-element.32), channel_id=1, source_target_pairs={{0,4},{4,0},{1,5},{5,1},{2,6},{6,2},{3,7},{7,3},{8,12},{12,8},{9,1... | collective-permute-start | bytes 479240 | tf_op jit(solution)/shard_map/ppermute | solution.py:247
  24.0 8.1 %collective-permute-start.8 = (bf16[24,3328]{1,0:T(8,128)(2,1)S(1)}, bf16[24,3328]{1,0:T(8,128)(2,1)S(1)}, u32[]{:S(2)}, u32[]{:S(2)}) collective-permute-start(bf16[24,3328]{1,0:T(8,128)(2,1)S(1)} %get-tuple-element.33), channel_id=1, source_target_pairs={{0,4},{4,0},{1,5},{5,1},{2,6},{6,2},{3,7},{7,3},{8,12},{12,8},{9,1... | collective-permute-start | bytes 479240 | tf_op jit(solution)/shard_map/ppermute | solution.py:247
  24.2 9.8 %collective-permute-start.14 = (bf16[24,6656]{1,0:T(8,128)(2,1)S(1)}, bf16[24,6656]{1,0:T(8,128)(2,1)S(1)}, u32[]{:S(2)}, u32[]{:S(2)}) collective-permute-start(bf16[24,6656]{1,0:T(8,128)(2,1)S(1)} %collective-permute-done.4.refs_1_.refs_2_.refs_10_), channel_id=1, source_target_pairs={{0,8},{8,0},{16,24},{24,16},{1,9},{9,1},{17,25},{25,17},{2,10},{10... | collective-permute-start | bytes 958472 | tf_op jit(solution)/shard_map/ppermute | solution.py:243
  31.4 3.3 %collective-permute-start.10 = (bf16[24,6656]{1,0:T(8,128)(2,1)S(1)}, bf16[24,6656]{1,0:T(8,128)(2,1)S(1)}, u32[]{:S(2)}, u32[]{:S(2)}) collective-permute-start(bf16[24,6656]{1,0:T(8,128)(2,1)S(1)} %copy-done), channel_id=1, source_target_pairs={{0,4},{4,0},{1,5},{5,1},{2,6},{6,2},{3,7},{7,3},{8,12},{12,8},{9,1... | collective-permute-start | bytes 958472 | tf_op jit(solution)/shard_map/ppermute | solution.py:247
  31.5 3.2 %collective-permute-start.12 = (bf16[24,6656]{1,0:T(8,128)(2,1)S(1)}, bf16[24,6656]{1,0:T(8,128)(2,1)S(1)}, u32[]{:S(2)}, u32[]{:S(2)}) collective-permute-start(bf16[24,6656]{1,0:T(8,128)(2,1)S(1)} %collective-permute-done.4.refs_1_.refs_2_.refs_10_), channel_id=1, source_target_pairs={{0,4},{4,0},{1,5},{5,1},{2,6},{6,2},{3,7},{7,3},{8,12},{12,8},{9,1... | collective-permute-start | bytes 958472 | tf_op jit(solution)/shard_map/ppermute | solution.py:247
  32.8 9.9 %collective-permute-start.9 = (bf16[2,24,3328]{2,1,0:T(8,128)(2,1)S(1)}, bf16[2,24,3328]{2,1,0:T(8,128)(2,1)S(1)}, u32[]{:S(2)}, u32[]{:S(2)}) collective-permute-start(bf16[2,24,3328]{2,1,0:T(8,128)(2,1)S(1)} %get-tuple-element.35), channel_id=1, source_target_pairs={{0,8},{8,0},{16,24},{24,16},{1,9},{9,1},{17,25},{25,17},{2,10},{10... | collective-permute-start | bytes 958472 | tf_op jit(solution)/shard_map/ppermute | solution.py:243
  34.0 11.2 %collective-permute-start.15 = (bf16[24,6656]{1,0:T(8,128)(2,1)S(1)}, bf16[24,6656]{1,0:T(8,128)(2,1)S(1)}, u32[]{:S(2)}, u32[]{:S(2)}) collective-permute-start(bf16[24,6656]{1,0:T(8,128)(2,1)S(1)} %collective-permute-done.14.refs_3_.refs_11_), channel_id=1, source_target_pairs={{0,4},{4,0},{1,5},{5,1},{2,6},{6,2},{3,7},{7,3},{8,12},{12,8},{9,1... | collective-permute-start | bytes 958472 | tf_op jit(solution)/shard_map/ppermute | solution.py:247
  42.8 10.0 %collective-permute-start.13 = (bf16[24,3328]{1,0:T(8,128)(2,1)S(1)}, bf16[24,3328]{1,0:T(8,128)(2,1)S(1)}, u32[]{:S(2)}, u32[]{:S(2)}) collective-permute-start(bf16[24,3328]{1,0:T(8,128)(2,1)S(1)} %shard_map.161), channel_id=1, source_target_pairs={{0,16},{8,24},{16,0},{24,8},{1,17},{9,25},{17,1},{25,9},{2,18},{10... | collective-permute-start | bytes 479240 | tf_op jit(solution)/shard_map/ppermute | solution.py:243
  52.9 8.7 %collective-permute-start.17 = (bf16[24,3328]{1,0:T(8,128)(2,1)S(1)}, bf16[24,3328]{1,0:T(8,128)(2,1)S(1)}, u32[]{:S(2)}, u32[]{:S(2)}) collective-permute-start(bf16[24,3328]{1,0:T(8,128)(2,1)S(1)} %shard_map.163.refs_0_), channel_id=1, source_target_pairs={{0,16},{8,24},{16,0},{24,8},{1,17},{9,25},{17,1},{25,9},{2,18},{10... | collective-permute-start | bytes 479240 | tf_op jit(solution)/shard_map/ppermute | solution.py:243
  52.9 9.5 %collective-permute-start.16 = (bf16[24,3328]{1,0:T(8,128)(2,1)S(1)}, bf16[24,3328]{1,0:T(8,128)(2,1)S(1)}, u32[]{:S(2)}, u32[]{:S(2)}) collective-permute-start(bf16[24,3328]{1,0:T(8,128)(2,1)S(1)} %shard_map.163.refs_0_), channel_id=1, source_target_pairs={{0,8},{8,0},{16,24},{24,16},{1,9},{9,1},{17,25},{25,17},{2,10},{10... | collective-permute-start | bytes 479240 | tf_op jit(solution)/shard_map/ppermute | solution.py:243
  62.5 5.3 %collective-permute-start.18 = (bf16[24,3328]{1,0:T(8,128)(2,1)S(1)}, bf16[24,3328]{1,0:T(8,128)(2,1)S(1)}, u32[]{:S(2)}, u32[]{:S(2)}) collective-permute-start(bf16[24,3328]{1,0:T(8,128)(2,1)S(1)} %shard_map.165.refs_2_), channel_id=1, source_target_pairs={{0,8},{8,0},{16,24},{24,16},{1,9},{9,1},{17,25},{25,17},{2,10},{10... | collective-permute-start | bytes 479240 | tf_op jit(solution)/shard_map/ppermute | solution.py:243
  62.8 5.0 %collective-permute-start.19 = (bf16[24,3328]{1,0:T(8,128)(2,1)S(1)}, bf16[24,3328]{1,0:T(8,128)(2,1)S(1)}, u32[]{:S(2)}, u32[]{:S(2)}) collective-permute-start(bf16[24,3328]{1,0:T(8,128)(2,1)S(1)} %shard_map.163.refs_0_), channel_id=1, source_target_pairs={{0,4},{4,0},{1,5},{5,1},{2,6},{6,2},{3,7},{7,3},{8,12},{12,8},{9,1... | collective-permute-start | bytes 479240 | tf_op jit(solution)/shard_map/ppermute | solution.py:247
  62.8 5.0 %collective-permute-start.21 = (bf16[24,3328]{1,0:T(8,128)(2,1)S(1)}, bf16[24,3328]{1,0:T(8,128)(2,1)S(1)}, u32[]{:S(2)}, u32[]{:S(2)}) collective-permute-start(bf16[24,3328]{1,0:T(8,128)(2,1)S(1)} %shard_map.165.refs_2_), channel_id=1, source_target_pairs={{0,4},{4,0},{1,5},{5,1},{2,6},{6,2},{3,7},{7,3},{8,12},{12,8},{9,1... | collective-permute-start | bytes 479240 | tf_op jit(solution)/shard_map/ppermute | solution.py:247
  63.3 4.5 %collective-permute-start.20 = (bf16[24,3328]{1,0:T(8,128)(2,1)S(1)}, bf16[24,3328]{1,0:T(8,128)(2,1)S(1)}, u32[]{:S(2)}, u32[]{:S(2)}) collective-permute-start(bf16[24,3328]{1,0:T(8,128)(2,1)S(1)} %collective-permute-done.16.refs_2_.refs_1_), channel_id=1, source_target_pairs={{0,4},{4,0},{1,5},{5,1},{2,6},{6,2},{3,7},{7,3},{8,12},{12,8},{9,1... | collective-permute-start | bytes 479240 | tf_op jit(solution)/shard_map/ppermute | solution.py:247
  83.0 14.6 %collective-permute-start.23 = (bf16[24,1024]{1,0:T(8,128)(2,1)S(1)}, bf16[24,1024]{1,0:T(8,128)(2,1)S(1)}, u32[]{:S(2)}, u32[]{:S(2)}) collective-permute-start(bf16[24,1024]{1,0:T(8,128)(2,1)S(1)} %get-tuple-element.42), channel_id=1, source_target_pairs={{0,1},{1,0},{2,3},{3,2},{4,5},{5,4},{6,7},{7,6},{8,9},{9,8},{10,11... | collective-permute-start | bytes 147464 | tf_op jit(solution)/shard_map/ppermute | solution.py:479
  84.5 13.1 %collective-permute-start.24 = (bf16[24,1024]{1,0:T(8,128)(2,1)S(1)}, bf16[24,1024]{1,0:T(8,128)(2,1)S(1)}, u32[]{:S(2)}, u32[]{:S(2)}) collective-permute-start(bf16[24,1024]{1,0:T(8,128)(2,1)S(1)} %get-tuple-element.43), channel_id=1, source_target_pairs={{0,2},{1,3},{2,0},{3,1},{4,6},{5,7},{6,4},{7,5},{8,10},{9,11},{10,... | collective-permute-start | bytes 147464 | tf_op jit(solution)/shard_map/ppermute | solution.py:479
  86.1 11.5 %collective-permute-start.25 = (bf16[24,1024]{1,0:T(8,128)(2,1)S(1)}, bf16[24,1024]{1,0:T(8,128)(2,1)S(1)}, u32[]{:S(2)}, u32[]{:S(2)}) collective-permute-start(bf16[24,1024]{1,0:T(8,128)(2,1)S(1)} %get-tuple-element.44), channel_id=1, source_target_pairs={{0,3},{1,2},{2,1},{3,0},{4,7},{5,6},{6,5},{7,4},{8,11},{9,10},{10,... | collective-permute-start | bytes 147464 | tf_op jit(solution)/shard_map/ppermute | solution.py:479
  (5 other events, 19.0 us)
